TPU v7x, 32 devices: a whole 2x2x4 slice. The times are simulated.
32 devices in a mesh: dp: 8 (over z, x), mp: 4 (over y, core).
Axes of the slice: x: 2, y: 2, z: 4, core: 2. Of those that a mesh axis runs over, the one named last changes fastest.
Arguments:
- tokens: bfloat16 [16, 1024, 1024], P('dp', 'mp'), may hold values from -6 to 6
- out_cot: float32 [16, 1024, 1024], P('dp', 'mp'), may hold values from -6 to 6
- cls_offset: int32 [16, 4], P('dp'), may hold values from 0 to 255
- w_qkv: float32 [1024, 3, 1024], P('dp', None, 'mp'), may hold values from -0.1875 to 0.1875
- w_out: float32 [1024, 1024], P('dp', 'mp'), may hold values from -3.5 to 3.5
- w_one: float32 [1024, 4096], P('dp', 'mp'), may hold values from -0.1875 to 0.1875
- w_two: float32 [1024, 4096], P('dp', 'mp'), may hold values from -0.16875 to 0.16875
- vectors: float32 [12, 1024], replicated, may hold values from -1 to 4
- m_qkv: float32 [1024, 3, 1024], P('dp', None, 'mp'), may hold values from -1.25 to 1.25
- v_qkv: float32 [1024, 3, 1024], P('dp', None, 'mp'), may hold values from 0.000589824 to 0.002359296
- m_out: float32 [1024, 1024], P('dp', 'mp'), may hold values from -0.5 to 0.5
- v_out: float32 [1024, 1024], P('dp', 'mp'), may hold values from 7.3728e-05 to 0.000294912
- m_one: float32 [1024, 4096], P('dp', 'mp'), may hold values from -1.25 to 1.25
- v_one: float32 [1024, 4096], P('dp', 'mp'), may hold values from 0.000589824 to 0.002359296
- m_two: float32 [1024, 4096], P('dp', 'mp'), may hold values from -1.25 to 1.25
- v_two: float32 [1024, 4096], P('dp', 'mp'), may hold values from 0.000589824 to 0.002359296
- m_vec: float32 [12, 1024], replicated, may hold values from -5 to 5
- v_vec: float32 [12, 1024], replicated, may hold values from 0.0098304 to 0.0393216
Outputs:
- pooled: float32 [16, 1024], P('dp', 'mp')
- input_grad: float32 [16, 1024, 1024], P('dp', 'mp')
- grad_norm: float32 [], replicated
- qkv_new: float32 [1024, 3, 1024], P('dp', None, 'mp')
- qkv_first: float32 [1024, 3, 1024], P('dp', None, 'mp')
- qkv_second: float32 [1024, 3, 1024], P('dp', None, 'mp')
- out_new: float32 [1024, 1024], P('dp', 'mp')
- out_first: float32 [1024, 1024], P('dp', 'mp')
- out_second: float32 [1024, 1024], P('dp', 'mp')
- one_new: float32 [1024, 4096], P('dp', 'mp')
- one_first: float32 [1024, 4096], P('dp', 'mp')
- one_second: float32 [1024, 4096], P('dp', 'mp')
- two_new: float32 [1024, 4096], P('dp', 'mp')
- two_first: float32 [1024, 4096], P('dp', 'mp')
- two_second: float32 [1024, 4096], P('dp', 'mp')
- vec_new: float32 [12, 1024], replicated
- vec_first: float32 [12, 1024], replicated
- vec_second: float32 [12, 1024], replicated
All inputs are finite; a program needn't handle non-finite values.
Results may differ from a plain program's by a relative error of at most 0.015.
The roundings to bfloat16 on the way count: a program that leaves them out, or rounds other values in their place, can miss the bound.
Values may be sent and summed in bfloat16 or wider, within the bound.
A program may use at most 128 MiB of HBM per device.

v0:
```python
from functools import partial
import math

import jax
import jax.numpy as jnp
from jax import lax
from jax.sharding import PartitionSpec as P

D = 1024
HD = 64
FF = 4096
DOC_LEN = 1024
CLS_GAP = 256
STEP = 10


norm_eps = 1e-05
beta_one = 0.9
beta_two = 0.999
adam_eps = 1e-08
weight_decay = 0.01
vector_rate = 0.4
highest = lax.Precision.HIGHEST
contract_last = (((1,), (1,)), ((), ()))


def layer_norm(values_in, scale_vec, shift_vec):
    row_mean = jnp.mean(values_in, axis=-1, keepdims=True)
    centered = values_in - row_mean
    row_var = jnp.mean(centered * centered, axis=-1, keepdims=True)
    return centered * lax.rsqrt(row_var + norm_eps) * scale_vec + shift_vec


def clip_limit(params_all, tokens_all):
    return 0.005 * math.sqrt(params_all * tokens_all)


def matrix_rates(model_width, hidden, length):
    out_fan = max(1, 3 * model_width // length)
    return (
        1.5 / math.sqrt(model_width),
        1.5 / math.sqrt(out_fan),
        1.5 / math.sqrt(model_width),
        1.5 / math.sqrt(hidden),
    )


def adam_update(parameter, gradient, first_old, second_old, step_rate, decay_rate):
    first_new = beta_one * first_old + (1.0 - beta_one) * gradient
    second_new = beta_two * second_old + (1.0 - beta_two) * gradient * gradient
    first_hat = first_new / (1.0 - beta_one**STEP)
    second_hat = second_new / (1.0 - beta_two**STEP)
    updated = parameter - step_rate * (
        first_hat / (jnp.sqrt(second_hat) + adam_eps) + decay_rate * parameter
    )
    return (updated, first_new, second_new)


def attend_forward(key_heads, value_heads, query_block):
    scores = jnp.einsum(
        "qhd,khd->hqk", query_block, key_heads, preferred_element_type=jnp.float32
    ) * HD ** (-0.5)
    row_top = jnp.max(scores, axis=-1, keepdims=True)
    raised = jnp.exp(scores - row_top)
    row_total = jnp.sum(raised, axis=-1, keepdims=True)
    shares = (raised / row_total).astype(jnp.bfloat16)
    mixed = jnp.einsum("hqk,khd->qhd", shares, value_heads, preferred_element_type=jnp.float32)
    return (mixed.astype(jnp.bfloat16), (row_top + jnp.log(row_total))[..., 0])


def attend_backward(key_heads, value_heads, carry, block):
    query_block, log_block, grad_block = block
    key_sum, value_sum = carry
    scores = jnp.einsum(
        "qhd,khd->hqk", query_block, key_heads, preferred_element_type=jnp.float32
    ) * HD ** (-0.5)
    shares = jnp.exp(scores - log_block[..., None])
    value_sum = value_sum + jnp.einsum(
        "hqk,qhd->khd", shares.astype(jnp.bfloat16), grad_block, preferred_element_type=jnp.float32
    )
    dshares = jnp.einsum(
        "qhd,khd->hqk", grad_block, value_heads, preferred_element_type=jnp.float32
    )
    dscores = (shares * (dshares - jnp.sum(shares * dshares, axis=-1, keepdims=True))).astype(
        jnp.bfloat16
    )
    query_grad = jnp.einsum(
        "hqk,khd->qhd", dscores, key_heads, preferred_element_type=jnp.float32
    ) * HD ** (-0.5)
    key_sum = key_sum + jnp.einsum(
        "hqk,qhd->khd", dscores, query_block, preferred_element_type=jnp.float32
    ) * HD ** (-0.5)
    return ((key_sum, value_sum), query_grad)


def local(
    tokens,
    out_cot,
    cls_offset,
    w_qkv,
    w_out,
    w_one,
    w_two,
    vectors,
    m_qkv,
    v_qkv,
    m_out,
    v_out,
    m_one,
    v_one,
    m_two,
    v_two,
    m_vec,
    v_vec,
):
    rows_dev = tokens.shape[1]
    model_width = tokens.shape[2]
    doc_length = rows_dev * lax.axis_size("mp")
    head_cols = w_qkv.shape[2]
    heads_dev = head_cols // HD
    ff_cols = w_one.shape[1]
    block_rows = min(512, doc_length)
    block_count = doc_length // block_rows
    rank_mp = lax.axis_index("mp")
    bias_flat = vectors[8:].reshape(-1)
    query_bias = lax.dynamic_slice_in_dim(vectors[0], rank_mp * head_cols, head_cols)
    value_bias = lax.dynamic_slice_in_dim(vectors[1], rank_mp * head_cols, head_cols)
    ff_bias = lax.dynamic_slice_in_dim(bias_flat, rank_mp * ff_cols, ff_cols)
    shards = (
        w_qkv.astype(jnp.bfloat16),
        w_out.astype(jnp.bfloat16),
        w_one.astype(jnp.bfloat16),
        w_two.astype(jnp.bfloat16),
    )

    def one_document(carry, inputs):
        sum_qkv, sum_out, sum_one, sum_two, sum_vec = carry
        doc_rows, doc_cot, doc_offset = inputs
        gathered = (
            lax.all_gather(shards[0], "dp", axis=0, tiled=True),
            lax.all_gather(shards[1], "dp", axis=0, tiled=True),
            lax.all_gather(shards[2], "dp", axis=0, tiled=True),
            lax.all_gather(shards[3], "dp", axis=0, tiled=True),
        )
        full_qkv, full_out, full_one, full_two = gathered
        rows_all = lax.all_gather(doc_rows, "mp", axis=0, tiled=True)
        projected = jnp.einsum(
            "te,ecf->tcf", rows_all, full_qkv, preferred_element_type=jnp.float32
        )
        queries = (projected[:, 0] + query_bias).astype(jnp.bfloat16)
        keys_all = projected[:, 1].astype(jnp.bfloat16)
        values_all = (projected[:, 2] + value_bias).astype(jnp.bfloat16)
        key_heads = keys_all.reshape(doc_length, heads_dev, HD)
        value_heads = values_all.reshape(doc_length, heads_dev, HD)
        query_blocks = queries.reshape(block_count, block_rows, heads_dev, HD)
        attended, log_sums = lax.map(partial(attend_forward, key_heads, value_heads), query_blocks)
        attended = attended.reshape(doc_length, head_cols)
        part_rows = attended
        branch = lax.psum_scatter(
            lax.dot_general(part_rows, full_out, contract_last, preferred_element_type=jnp.float32),
            "mp",
            scatter_dimension=0,
            tiled=True,
        )
        z_one = doc_rows.astype(jnp.float32) + branch + vectors[2]
        y_one, first_back = jax.vjp(layer_norm, z_one, vectors[3], vectors[4])
        normed_all = lax.all_gather(y_one.astype(jnp.bfloat16), "mp", axis=0, tiled=True)
        pre_act = jnp.dot(normed_all, full_one, preferred_element_type=jnp.float32) + ff_bias
        hidden = jax.nn.gelu(pre_act, approximate=False).astype(jnp.bfloat16)
        part_rows = hidden
        ffn_out = lax.psum_scatter(
            lax.dot_general(part_rows, full_two, contract_last, preferred_element_type=jnp.float32),
            "mp",
            scatter_dimension=0,
            tiled=True,
        )
        z_two = y_one + ffn_out + vectors[5]
        layer_out, second_back = jax.vjp(layer_norm, z_two, vectors[6], vectors[7])
        positions = doc_offset + jnp.arange(doc_offset.shape[0], dtype=jnp.int32) * CLS_GAP
        row_ids = rank_mp * rows_dev + jnp.arange(rows_dev, dtype=jnp.int32)
        picks = (
            jnp.sum((positions[:, None] == row_ids[None, :]).astype(jnp.float32), axis=0)
            / doc_offset.shape[0]
        )
        pool_part = jnp.dot(picks, layer_out, precision=highest)
        dz_two, dscale_two, dshift_two = second_back(doc_cot)
        dffn_all = lax.all_gather(dz_two.astype(jnp.bfloat16), "mp", axis=0, tiled=True)
        grad_two = jnp.einsum("td,tf->df", dffn_all, hidden, preferred_element_type=jnp.float32)
        dhidden = jnp.dot(dffn_all, full_two, preferred_element_type=jnp.float32)
        gelu_back = jax.vjp(partial(jax.nn.gelu, approximate=False), pre_act)[1]
        dpre = gelu_back(dhidden)[0].astype(jnp.bfloat16)
        grad_one = jnp.einsum("td,tf->df", normed_all, dpre, preferred_element_type=jnp.float32)
        dff_bias = jnp.sum(dpre, axis=0, dtype=jnp.float32)
        part_rows = dpre
        dy_branch = lax.psum_scatter(
            lax.dot_general(part_rows, full_one, contract_last, preferred_element_type=jnp.float32),
            "mp",
            scatter_dimension=0,
            tiled=True,
        )
        dz_one, dscale_one, dshift_one = first_back(dz_two + dy_branch)
        dbranch_all = lax.all_gather(dz_one.astype(jnp.bfloat16), "mp", axis=0, tiled=True)
        grad_out = jnp.einsum(
            "td,tf->df", dbranch_all, attended, preferred_element_type=jnp.float32
        )
        dattended = jnp.dot(dbranch_all, full_out, preferred_element_type=jnp.float32).astype(
            jnp.bfloat16
        )
        grad_blocks = dattended.reshape(block_count, block_rows, heads_dev, HD)
        zero_heads = jnp.zeros((doc_length, heads_dev, HD), jnp.float32)
        (key_sum, value_sum), query_grad = lax.scan(
            partial(attend_backward, key_heads, value_heads),
            (zero_heads, zero_heads),
            (query_blocks, log_sums, grad_blocks),
        )
        dprojected = jnp.stack(
            [
                query_grad.reshape(doc_length, head_cols),
                key_sum.reshape(doc_length, head_cols),
                value_sum.reshape(doc_length, head_cols),
            ],
            axis=1,
        ).astype(jnp.bfloat16)
        grad_qkv = jnp.einsum(
            "te,tcf->ecf", rows_all, dprojected, preferred_element_type=jnp.float32
        )
        part_rows = dprojected
        dx_branch = lax.psum_scatter(
            jnp.einsum(
                "tcf,ecf->te", part_rows, full_qkv, preferred_element_type=jnp.float32
            ).astype(jnp.bfloat16),
            "mp",
            scatter_dimension=0,
            tiled=True,
        ).astype(jnp.float32)
        input_rows = dz_one + dx_branch
        head_sums = jnp.sum(dprojected, axis=0, dtype=jnp.float32)
        vec_local = jnp.zeros_like(vectors)
        vec_local = lax.dynamic_update_slice(
            vec_local, head_sums[0][None, :], (0, rank_mp * head_cols)
        )
        vec_local = lax.dynamic_update_slice(
            vec_local, head_sums[2][None, :], (1, rank_mp * head_cols)
        )
        plain_rows = jnp.stack(
            [
                jnp.sum(dz_one, axis=0),
                dscale_one,
                dshift_one,
                jnp.sum(dz_two, axis=0),
                dscale_two,
                dshift_two,
            ]
        )
        vec_local = vec_local.at[2:8].set(plain_rows)
        ff_spread = lax.dynamic_update_slice(
            jnp.zeros_like(bias_flat), dff_bias, (rank_mp * ff_cols,)
        )
        vec_local = vec_local.at[8:].set(ff_spread.reshape(-1, model_width))
        new_carry = (
            sum_qkv + grad_qkv,
            sum_out + grad_out,
            sum_one + grad_one,
            sum_two + grad_two,
            sum_vec + vec_local,
        )
        return (new_carry, (input_rows, pool_part))

    start_carry = (
        jnp.zeros((model_width, 3, head_cols), jnp.float32),
        jnp.zeros((model_width, head_cols), jnp.float32),
        jnp.zeros((model_width, ff_cols), jnp.float32),
        jnp.zeros((model_width, ff_cols), jnp.float32),
        jnp.zeros_like(vectors),
    )
    final_carry, outputs = lax.scan(one_document, start_carry, (tokens, out_cot, cls_offset))
    sum_qkv, sum_out, sum_one, sum_two, sum_vec = final_carry
    input_grad, pool_parts = outputs
    pooled = lax.psum_scatter(pool_parts, "mp", scatter_dimension=1, tiled=True)
    g_qkv, g_out, g_one, g_two = (
        lax.psum_scatter(sum_qkv, "dp", scatter_dimension=0, tiled=True),
        lax.psum_scatter(sum_out, "dp", scatter_dimension=0, tiled=True),
        lax.psum_scatter(sum_one, "dp", scatter_dimension=0, tiled=True),
        lax.psum_scatter(sum_two, "dp", scatter_dimension=0, tiled=True),
    )
    own_squares = (
        jnp.sum(g_qkv * g_qkv)
        + jnp.sum(g_out * g_out)
        + jnp.sum(g_one * g_one)
        + jnp.sum(g_two * g_two)
    )
    g_vec, squares_all = lax.psum((sum_vec, own_squares), ("dp", "mp"))
    grad_norm = jnp.sqrt(squares_all + jnp.sum(g_vec * g_vec))
    tokens_all = tokens.shape[0] * doc_length * lax.axis_size("dp")
    factor = jnp.minimum(1.0, clip_limit(4 * D * D + 2 * D * FF, tokens_all) / (grad_norm + 1e-06))
    rates = matrix_rates(D, FF, DOC_LEN)
    qkv_new, qkv_first, qkv_second = adam_update(
        w_qkv, g_qkv * factor, m_qkv, v_qkv, rates[0], weight_decay
    )
    out_new, out_first, out_second = adam_update(
        w_out, g_out * factor, m_out, v_out, rates[1], weight_decay
    )
    one_new, one_first, one_second = adam_update(
        w_one, g_one * factor, m_one, v_one, rates[2], weight_decay
    )
    two_new, two_first, two_second = adam_update(
        w_two, g_two * factor, m_two, v_two, rates[3], weight_decay
    )
    vec_new, vec_first, vec_second = adam_update(
        vectors, g_vec * factor, m_vec, v_vec, vector_rate, 0.0
    )
    return (
        pooled,
        input_grad,
        grad_norm,
        qkv_new,
        qkv_first,
        qkv_second,
        out_new,
        out_first,
        out_second,
        one_new,
        one_first,
        one_second,
        two_new,
        two_first,
        two_second,
        vec_new,
        vec_first,
        vec_second,
    )


def solution(mesh):
    placed = (
        P("dp", "mp", None),
        P("dp", "mp", None),
        P("dp", None),
        P("dp", None, "mp"),
        P("dp", "mp"),
        P("dp", "mp"),
        P("dp", "mp"),
        P(),
        P("dp", None, "mp"),
        P("dp", None, "mp"),
        P("dp", "mp"),
        P("dp", "mp"),
        P("dp", "mp"),
        P("dp", "mp"),
        P("dp", "mp"),
        P("dp", "mp"),
        P(),
        P(),
    )
    return jax.shard_map(
        local,
        mesh=mesh,
        in_specs=placed,
        out_specs=(
            P("dp", "mp"),
            P("dp", "mp", None),
            P(),
            P("dp", None, "mp"),
            P("dp", None, "mp"),
            P("dp", None, "mp"),
            P("dp", "mp"),
            P("dp", "mp"),
            P("dp", "mp"),
            P("dp", "mp"),
            P("dp", "mp"),
            P("dp", "mp"),
            P("dp", "mp"),
            P("dp", "mp"),
            P("dp", "mp"),
            P(),
            P(),
            P(),
        ),
        check_vma=False,
    )
```

profile of v0, /device:TPU:0, one launch (start us, length us, event | category | flops | bytes accessed | tf_op | source)
XLA Modules:
  0.0 1452.4 jit_solution(16024585275694158594)
XLA Ops:
  16.4 1021.1 %while.95 = (s32[]{:T(128)}, f32[1024,3,256]{2,0,1:T(8,128)}, f32[1024,256]{1,0:T(8,128)}, f32[1024,1024]{1,0:T(8,128)}, f32[1024,1024]{1,0:T(8,128)}, /*index=5...) while((s32[]{:T(128)}, f32[1024,3,256]{2,0,1:T(8,128)}, ...), condition=%wide.region_29.30_spmd.clone, body=%wide.region_0.29_spmd.clone.sunk | while | flops 21378385920 | bytes 483157248 | solution.py:276
  20.7 35.9 %all_gather.71 = bf16[1024,256]{1,0:T(8,128)(2,1)} all-gather(bf16[128,256]{1,0:T(8,128)(2,1)} %get-tuple-element.1215), channel_id=1, replica_groups=mesh['dp'=8,'mp'=4] {'dp'}, dimensions={0}, use_global_device_ids=true | all-gather | bytes 589824 | tf_op jit(solution)/shard_map/while/body/eval_jaxpr/all_gather | solution.py:141
  56.6 13.1 all-gather.14.cloned.1.call-done
  69.7 23.4 %all-gather.12.cloned.1.call-done = bf16[1,1024,1024]{2,1,0:T(8,128)(2,1)} async-done(((bf16[1,256,1024]{2,1,0:T(8,128)(2,1)}), bf16[1,1024,1024]{2,1,0:T(8,128)(2,1)}) %all-gather.12.cloned.1.call-update) | async-done | bytes 2097168 | tf_op jit(solution)/shard_map/while/body/eval_jaxpr/all_gather | solution.py:146
  93.1 3.9 fusion.203
  100.8 12.3 while.96
  115.7 2.7 fusion.207
  120.7 42.4 %reduce-scatter.22.cloned.1.call-done = f32[256,1024]{1,0:T(8,128)} async-done(((f32[1024,1024]{1,0:T(8,128)}), f32[256,1024]{1,0:T(8,128)}) %reduce-scatter.22.cloned.1.call-update) | async-done | bytes 1048592 | tf_op jit(solution)/shard_map/while/body/eval_jaxpr/reduce_scatter | solution.py:159
  167.2 48.1 %all-gather.18.cloned.1.call-done = bf16[1024,1024]{1,0:T(8,128)(2,1)} async-done(((bf16[128,1024]{1,0:T(8,128)(2,1)}), bf16[1024,1024]{1,0:T(8,128)(2,1)}) %all-gather.18.cloned.1.call-update) | async-done | bytes 2097168 | tf_op jit(solution)/shard_map/while/body/eval_jaxpr/all_gather | solution.py:142
  215.2 23.2 %all-gather.16.cloned.1.call-done = bf16[1024,1024]{1,0:T(8,128)(2,1)} async-done(((bf16[256,1024]{1,0:T(8,128)(2,1)}), bf16[1024,1024]{1,0:T(8,128)(2,1)}) %all-gather.16.cloned.1.call-update) | async-done | bytes 2097168 | tf_op jit(solution)/shard_map/while/body/eval_jaxpr/all_gather | solution.py:167
  238.4 14.9 %multiply_convert_fusion.4 = (bf16[1024,1024]{1,0:T(8,128)(2,1)}, f32[1024,1024]{1,0:T(8,128)}, f32[1024,1024]{1,0:T(8,128)}) fusion(f32[1024]{0:T(1024)S(1)} %get-tuple-element.1217, bf16[1024,1024]{1,0:T(8,128)(2,1)} %all-gather.16.cloned.1.call-done, bf16[1024,1024]{1,0:T(8,128)(2,1)} %all-gather.18.cloned.1.call-done), kind=kOutput, calls=%fused_computation.52.clone.1 | convolution fusion | flops 2216689664 | bytes 14684160 | tf_op jit(solution)/shard_map/while/body/eval_jaxpr/dot_general | solution.py:168
  253.3 37.2 %all-gather.20.cloned.1.call-done = bf16[1024,1024]{1,0:T(8,128)(2,1)} async-done(((bf16[128,1024]{1,0:T(8,128)(2,1)}), bf16[1024,1024]{1,0:T(8,128)(2,1)}) %all-gather.20.cloned.1.call-update) | async-done | bytes 2097168 | tf_op jit(solution)/shard_map/while/body/eval_jaxpr/all_gather | solution.py:143
  290.5 6.5 fusion.211
  297.1 43.1 %reduce-scatter.24.cloned.1.call-done = f32[256,1024]{1,0:T(8,128)} async-done(((f32[1024,1024]{1,0:T(8,128)}), f32[256,1024]{1,0:T(8,128)}) %reduce-scatter.24.cloned.1.call-update) | async-done | bytes 1048592 | tf_op jit(solution)/shard_map/while/body/eval_jaxpr/reduce_scatter | solution.py:171
  344.5 22.7 %all-gather.22.cloned.1.call-done = bf16[1024,1024]{1,0:T(8,128)(2,1)} async-done(((bf16[256,1024]{1,0:T(8,128)(2,1)}), bf16[1024,1024]{1,0:T(8,128)(2,1)}) %all-gather.22.cloned.1.call-update) | async-done | bytes 2097168 | tf_op jit(solution)/shard_map/while/body/eval_jaxpr/all_gather | solution.py:187
  367.2 8.4 convert_reduce_fusion.6
  376.9 4.3 fusion.216
  381.4 44.6 %reduce-scatter.26.cloned.1.call-done = f32[256,1024]{1,0:T(8,128)} async-done(((f32[1024,1024]{1,0:T(8,128)}), f32[256,1024]{1,0:T(8,128)}) %reduce-scatter.26.cloned.1.call-update) | async-done | bytes 1048592 | tf_op jit(solution)/shard_map/while/body/eval_jaxpr/reduce_scatter | solution.py:195
  430.4 22.5 %all-gather.24.cloned.1.call-done = bf16[1024,1024]{1,0:T(8,128)(2,1)} async-done(((bf16[256,1024]{1,0:T(8,128)(2,1)}), bf16[1024,1024]{1,0:T(8,128)(2,1)}) %all-gather.24.cloned.1.call-update) | async-done | bytes 2097168 | tf_op jit(solution)/shard_map/while/body/eval_jaxpr/all_gather | solution.py:202
  452.9 3.2 convolution_convert_fusion.2
  456.1 2.8 reshape.319
  461.1 21.3 %while.97 = (s32[]{:T(128)}, f32[1024,4,64]{0,2,1:T(8,128)S(1)}, f32[1024,4,64]{0,2,1:T(8,128)S(1)}, bf16[2,512,4,64]{1,3,2,0:T(8,128)(2,1)}, bf16[2,512,4,64]{1...) while((s32[]{:T(128)}, f32[1024,4,64]{0,2,1:T(8,128)S(1)}, ...), condition=%wide.region_18.18_spmd.clone, body=%wide.region_16.17_spmd.clone.sunk | while | flops 1368782848 | bytes 78700808 | solution.py:211
  464.4 2.8 multiply_reduce_fusion.21
  475.1 2.8 multiply_reduce_fusion.21
  487.6 5.2 bitcast_convert_fusion.2
  494.5 6.7 select_add_fusion.10
  501.2 4.4 select_add_fusion.9
  510.1 3.6 select_add_fusion.8
  513.7 10.7 reduce-scatter.28.cloned.1.call-done
  531.1 34.2 %all_gather.71 = bf16[1024,256]{1,0:T(8,128)(2,1)} all-gather(bf16[128,256]{1,0:T(8,128)(2,1)} %get-tuple-element.1215), channel_id=1, replica_groups=mesh['dp'=8,'mp'=4] {'dp'}, dimensions={0}, use_global_device_ids=true | all-gather | bytes 589824 | tf_op jit(solution)/shard_map/while/body/eval_jaxpr/all_gather | solution.py:141
  565.3 12.2 all-gather.14.cloned.1.call-done
  577.5 23.4 %all-gather.12.cloned.1.call-done = bf16[1,1024,1024]{2,1,0:T(8,128)(2,1)} async-done(((bf16[1,256,1024]{2,1,0:T(8,128)(2,1)}), bf16[1,1024,1024]{2,1,0:T(8,128)(2,1)}) %all-gather.12.cloned.1.call-update) | async-done | bytes 2097168 | tf_op jit(solution)/shard_map/while/body/eval_jaxpr/all_gather | solution.py:146
  600.9 3.9 fusion.203
  608.6 12.3 while.96
  623.5 2.7 fusion.207
  628.5 42.4 %reduce-scatter.22.cloned.1.call-done = f32[256,1024]{1,0:T(8,128)} async-done(((f32[1024,1024]{1,0:T(8,128)}), f32[256,1024]{1,0:T(8,128)}) %reduce-scatter.22.cloned.1.call-update) | async-done | bytes 1048592 | tf_op jit(solution)/shard_map/while/body/eval_jaxpr/reduce_scatter | solution.py:159
  674.6 48.5 %all-gather.18.cloned.1.call-done = bf16[1024,1024]{1,0:T(8,128)(2,1)} async-done(((bf16[128,1024]{1,0:T(8,128)(2,1)}), bf16[1024,1024]{1,0:T(8,128)(2,1)}) %all-gather.18.cloned.1.call-update) | async-done | bytes 2097168 | tf_op jit(solution)/shard_map/while/body/eval_jaxpr/all_gather | solution.py:142
  723.0 23.2 %all-gather.16.cloned.1.call-done = bf16[1024,1024]{1,0:T(8,128)(2,1)} async-done(((bf16[256,1024]{1,0:T(8,128)(2,1)}), bf16[1024,1024]{1,0:T(8,128)(2,1)}) %all-gather.16.cloned.1.call-update) | async-done | bytes 2097168 | tf_op jit(solution)/shard_map/while/body/eval_jaxpr/all_gather | solution.py:167
  746.2 14.9 %multiply_convert_fusion.4 = (bf16[1024,1024]{1,0:T(8,128)(2,1)}, f32[1024,1024]{1,0:T(8,128)}, f32[1024,1024]{1,0:T(8,128)}) fusion(f32[1024]{0:T(1024)S(1)} %get-tuple-element.1217, bf16[1024,1024]{1,0:T(8,128)(2,1)} %all-gather.16.cloned.1.call-done, bf16[1024,1024]{1,0:T(8,128)(2,1)} %all-gather.18.cloned.1.call-done), kind=kOutput, calls=%fused_computation.52.clone.1 | convolution fusion | flops 2216689664 | bytes 14684160 | tf_op jit(solution)/shard_map/while/body/eval_jaxpr/dot_general | solution.py:168
  761.1 37.2 %all-gather.20.cloned.1.call-done = bf16[1024,1024]{1,0:T(8,128)(2,1)} async-done(((bf16[128,1024]{1,0:T(8,128)(2,1)}), bf16[1024,1024]{1,0:T(8,128)(2,1)}) %all-gather.20.cloned.1.call-update) | async-done | bytes 2097168 | tf_op jit(solution)/shard_map/while/body/eval_jaxpr/all_gather | solution.py:143
  798.3 6.5 fusion.211
  804.9 43.1 %reduce-scatter.24.cloned.1.call-done = f32[256,1024]{1,0:T(8,128)} async-done(((f32[1024,1024]{1,0:T(8,128)}), f32[256,1024]{1,0:T(8,128)}) %reduce-scatter.24.cloned.1.call-update) | async-done | bytes 1048592 | tf_op jit(solution)/shard_map/while/body/eval_jaxpr/reduce_scatter | solution.py:171
  852.3 22.7 %all-gather.22.cloned.1.call-done = bf16[1024,1024]{1,0:T(8,128)(2,1)} async-done(((bf16[256,1024]{1,0:T(8,128)(2,1)}), bf16[1024,1024]{1,0:T(8,128)(2,1)}) %all-gather.22.cloned.1.call-update) | async-done | bytes 2097168 | tf_op jit(solution)/shard_map/while/body/eval_jaxpr/all_gather | solution.py:187
  875.0 8.4 convert_reduce_fusion.6
  884.7 4.3 fusion.216
  889.2 44.6 %reduce-scatter.26.cloned.1.call-done = f32[256,1024]{1,0:T(8,128)} async-done(((f32[1024,1024]{1,0:T(8,128)}), f32[256,1024]{1,0:T(8,128)}) %reduce-scatter.26.cloned.1.call-update) | async-done | bytes 1048592 | tf_op jit(solution)/shard_map/while/body/eval_jaxpr/reduce_scatter | solution.py:195
  938.2 22.5 %all-gather.24.cloned.1.call-done = bf16[1024,1024]{1,0:T(8,128)(2,1)} async-done(((bf16[256,1024]{1,0:T(8,128)(2,1)}), bf16[1024,1024]{1,0:T(8,128)(2,1)}) %all-gather.24.cloned.1.call-update) | async-done | bytes 2097168 | tf_op jit(solution)/shard_map/while/body/eval_jaxpr/all_gather | solution.py:202
  960.7 3.2 convolution_convert_fusion.2
  963.8 2.8 reshape.319
  968.9 21.3 %while.97 = (s32[]{:T(128)}, f32[1024,4,64]{0,2,1:T(8,128)S(1)}, f32[1024,4,64]{0,2,1:T(8,128)S(1)}, bf16[2,512,4,64]{1,3,2,0:T(8,128)(2,1)}, bf16[2,512,4,64]{1...) while((s32[]{:T(128)}, f32[1024,4,64]{0,2,1:T(8,128)S(1)}, ...), condition=%wide.region_18.18_spmd.clone, body=%wide.region_16.17_spmd.clone.sunk | while | flops 1368782848 | bytes 78700808 | solution.py:211
  972.2 2.8 multiply_reduce_fusion.21
  982.8 2.8 multiply_reduce_fusion.21
  995.4 5.2 bitcast_convert_fusion.2
  1002.4 7.9 select_add_fusion.10
  1010.4 6.8 select_add_fusion.9
  1019.8 3.1 convolution_add_fusion.2
  1023.0 5.6 select_add_fusion.8
  1028.6 3.5 reduce-scatter.28.cloned.1.call-done
  1042.0 20.6 %reduce-scatter.20.cloned.1.call-done = f32[256,2]{1,0:T(8,128)} async-done(((f32[1024,2]{1,0:T(8,128)}), f32[256,2]{1,0:T(8,128)}) %reduce-scatter.20.cloned.1.call-update) | async-done | bytes 2064
  1064.2 65.7 %reduce-scatter.14.cloned.1.call-done = f32[128,256]{1,0:T(8,128)} async-done(((f32[1024,256]{1,0:T(8,128)}), f32[128,256]{1,0:T(8,128)}) %reduce-scatter.14.cloned.1.call-update) | async-done | bytes 131088 | tf_op jit(solution)/shard_map/reduce_scatter | solution.py:282
  1131.4 75.6 %reduce-scatter.12.cloned.1.call-done = f32[128,3,256]{2,0,1:T(8,128)} async-done(((f32[1024,3,256]{2,0,1:T(8,128)}), f32[128,3,256]{2,0,1:T(8,128)}) %reduce-scatter.12.cloned.1.call-update) | async-done | bytes 393232 | tf_op jit(solution)/shard_map/reduce_scatter | solution.py:281
  1210.0 87.5 %reduce-scatter.16.cloned.1.call-done = f32[128,1024]{1,0:T(8,128)} async-done(((f32[1024,1024]{1,0:T(8,128)}), f32[128,1024]{1,0:T(8,128)}) %reduce-scatter.16.cloned.1.call-update) | async-done | bytes 524304 | tf_op jit(solution)/shard_map/reduce_scatter | solution.py:283
  1300.0 89.2 %reduce-scatter.18.cloned.1.call-done = f32[128,1024]{1,0:T(8,128)} async-done(((f32[1024,1024]{1,0:T(8,128)}), f32[128,1024]{1,0:T(8,128)}) %reduce-scatter.18.cloned.1.call-update) | async-done | bytes 524304 | tf_op jit(solution)/shard_map/reduce_scatter | solution.py:284
  1391.6 41.0 %all-reduce = (f32[]{:T(128)}, f32[12,1024]{1,0:T(8,128)S(1)}) all-reduce(f32[]{:T(128)S(6)} %add.418, f32[12,1024]{1,0:T(8,128)S(1)} %copy-done.25), channel_id=1, replica_groups=mesh['dp'=8,'mp'=4] {'dp','mp'}, use_global_device_ids=true, to_apply=%region_39.40 | all-reduce | flops 12289 | bytes 98312 | tf_op jit(solution)/shard_map/psum | solution.py:292
  (435 shorter events, 168.3 us)
Async XLA Ops:
  16.4 80.5 %copy-start.21 = (bf16[128,1024]{1,0:T(8,128)(2,1)}, bf16[128,1024]{1,0:T(8,128)(2,1)S(1)}, u32[]{:S(2)}) copy-start(bf16[128,1024]{1,0:T(8,128)(2,1)S(1)} %get-tuple-element.1216) | copy-start | bytes 786436 | tf_op jit(solution)/shard_map/while
  16.4 53.2 %all-gather.14.cloned.1.call-start = ((), (), s32[]{:S(2)}) async-start(), calls=%async_computation.15 | async-start | bytes 1769472 | tf_op jit(solution)/shard_map/while/body/eval_jaxpr/all_gather | solution.py:140
  17.2 76.0 %all-gather.12.cloned.1.call-start = ((), (), s32[]{:S(2)}) async-start(), calls=%async_computation.14 | async-start | bytes 2621440 | tf_op jit(solution)/shard_map/while/body/eval_jaxpr/all_gather | solution.py:146
  19.1 144.0 %reduce-scatter.22.cloned.1.call-start = ((), (), s32[]{:S(2)}) async-start(), calls=%async_computation.16 | async-start | bytes 5242880 | tf_op jit(solution)/shard_map/while/body/eval_jaxpr/reduce_scatter | solution.py:159
  100.8 15.0 %copy-start.13 = (bf16[1024,256]{1,0:T(8,128)(2,1)S(1)}, bf16[1024,256]{1,0:T(8,128)(2,1)}, u32[]{:S(2)}) copy-start(bf16[1024,256]{1,0:T(8,128)(2,1)} %all_gather.71) | copy-start | bytes 1572868 | tf_op jit(solution)/shard_map/while
  115.7 47.4 %copy-start.16 = (bf16[2,256,1024]{2,1,0:T(8,128)(2,1)S(1)}, bf16[2,256,1024]{2,1,0:T(8,128)(2,1)}, u32[]{:S(2)}) copy-start(bf16[2,256,1024]{2,1,0:T(8,128)(2,1)} %get-tuple-element.1209) | copy-start | bytes 3145732 | tf_op jit(solution)/shard_map/while
  118.5 96.7 %all-gather.18.cloned.1.call-start = ((), (), s32[]{:S(2)}) async-start(), calls=%async_computation.18 | async-start | bytes 2359296 | tf_op jit(solution)/shard_map/while/body/eval_jaxpr/all_gather | solution.py:142
  119.1 119.3 %all-gather.16.cloned.1.call-start = ((), (), s32[]{:S(2)}) async-start(), calls=%async_computation.17 | async-start | bytes 2621440 | tf_op jit(solution)/shard_map/while/body/eval_jaxpr/all_gather | solution.py:167
  166.0 124.6 %all-gather.20.cloned.1.call-start = ((), (), s32[]{:S(2)}) async-start(), calls=%async_computation.19 | async-start | bytes 2359296 | tf_op jit(solution)/shard_map/while/body/eval_jaxpr/all_gather | solution.py:143
  166.5 173.7 %reduce-scatter.24.cloned.1.call-start = ((), (), s32[]{:S(2)}) async-start(), calls=%async_computation.20 | async-start | bytes 5242880 | tf_op jit(solution)/shard_map/while/body/eval_jaxpr/reduce_scatter | solution.py:171
  297.1 70.1 %all-gather.22.cloned.1.call-start = ((), (), s32[]{:S(2)}) async-start(), calls=%async_computation.21 | async-start | bytes 2621440 | tf_op jit(solution)/shard_map/while/body/eval_jaxpr/all_gather | solution.py:187
  344.4 81.6 %reduce-scatter.26.cloned.1.call-start = ((), (), s32[]{:S(2)}) async-start(), calls=%async_computation.22 | async-start | bytes 5242880 | tf_op jit(solution)/shard_map/while/body/eval_jaxpr/reduce_scatter | solution.py:195
  367.2 9.8 copy-start.44
  381.3 71.6 %all-gather.24.cloned.1.call-start = ((), (), s32[]{:S(2)}) async-start(), calls=%async_computation.23 | async-start | bytes 2621440 | tf_op jit(solution)/shard_map/while/body/eval_jaxpr/all_gather | solution.py:202
  430.2 94.2 %reduce-scatter.28.cloned.1.call-start = ((), (), s32[]{:S(2)}) async-start(), calls=%async_computation.24 | async-start | bytes 2621440 | tf_op jit(solution)/shard_map/while/body/eval_jaxpr/reduce_scatter | solution.py:228
  494.1 7.1 copy-start.41
  501.2 6.9 copy-start.23
  501.2 6.9 copy-start.7
  501.2 6.9 copy-start.11
  510.1 14.3 copy-start.6
  510.1 16.4 %copy-start.22 = (bf16[128,1024]{1,0:T(8,128)(2,1)S(1)}, bf16[128,1024]{1,0:T(8,128)(2,1)}, u32[]{:S(2)}) copy-start(bf16[128,1024]{1,0:T(8,128)(2,1)} %copy-done.21) | copy-start | bytes 786436 | tf_op jit(solution)/shard_map/while
  527.0 77.8 %copy-start.21 = (bf16[128,1024]{1,0:T(8,128)(2,1)}, bf16[128,1024]{1,0:T(8,128)(2,1)S(1)}, u32[]{:S(2)}) copy-start(bf16[128,1024]{1,0:T(8,128)(2,1)S(1)} %get-tuple-element.1216) | copy-start | bytes 786436 | tf_op jit(solution)/shard_map/while
  527.0 50.5 %all-gather.14.cloned.1.call-start = ((), (), s32[]{:S(2)}) async-start(), calls=%async_computation.15 | async-start | bytes 1769472 | tf_op jit(solution)/shard_map/while/body/eval_jaxpr/all_gather | solution.py:140
  527.6 73.4 %all-gather.12.cloned.1.call-start = ((), (), s32[]{:S(2)}) async-start(), calls=%async_computation.14 | async-start | bytes 2621440 | tf_op jit(solution)/shard_map/while/body/eval_jaxpr/all_gather | solution.py:146
  529.5 141.4 %reduce-scatter.22.cloned.1.call-start = ((), (), s32[]{:S(2)}) async-start(), calls=%async_computation.16 | async-start | bytes 5242880 | tf_op jit(solution)/shard_map/while/body/eval_jaxpr/reduce_scatter | solution.py:159
  608.6 15.0 %copy-start.13 = (bf16[1024,256]{1,0:T(8,128)(2,1)S(1)}, bf16[1024,256]{1,0:T(8,128)(2,1)}, u32[]{:S(2)}) copy-start(bf16[1024,256]{1,0:T(8,128)(2,1)} %all_gather.71) | copy-start | bytes 1572868 | tf_op jit(solution)/shard_map/while
  623.5 47.4 %copy-start.16 = (bf16[2,256,1024]{2,1,0:T(8,128)(2,1)S(1)}, bf16[2,256,1024]{2,1,0:T(8,128)(2,1)}, u32[]{:S(2)}) copy-start(bf16[2,256,1024]{2,1,0:T(8,128)(2,1)} %get-tuple-element.1209) | copy-start | bytes 3145732 | tf_op jit(solution)/shard_map/while
  626.3 96.7 %all-gather.18.cloned.1.call-start = ((), (), s32[]{:S(2)}) async-start(), calls=%async_computation.18 | async-start | bytes 2359296 | tf_op jit(solution)/shard_map/while/body/eval_jaxpr/all_gather | solution.py:142
  626.9 119.3 %all-gather.16.cloned.1.call-start = ((), (), s32[]{:S(2)}) async-start(), calls=%async_computation.17 | async-start | bytes 2621440 | tf_op jit(solution)/shard_map/while/body/eval_jaxpr/all_gather | solution.py:167
  673.8 124.6 %all-gather.20.cloned.1.call-start = ((), (), s32[]{:S(2)}) async-start(), calls=%async_computation.19 | async-start | bytes 2359296 | tf_op jit(solution)/shard_map/while/body/eval_jaxpr/all_gather | solution.py:143
  674.3 173.7 %reduce-scatter.24.cloned.1.call-start = ((), (), s32[]{:S(2)}) async-start(), calls=%async_computation.20 | async-start | bytes 5242880 | tf_op jit(solution)/shard_map/while/body/eval_jaxpr/reduce_scatter | solution.py:171
  804.9 70.1 %all-gather.22.cloned.1.call-start = ((), (), s32[]{:S(2)}) async-start(), calls=%async_computation.21 | async-start | bytes 2621440 | tf_op jit(solution)/shard_map/while/body/eval_jaxpr/all_gather | solution.py:187
  852.2 81.5 %reduce-scatter.26.cloned.1.call-start = ((), (), s32[]{:S(2)}) async-start(), calls=%async_computation.22 | async-start | bytes 5242880 | tf_op jit(solution)/shard_map/while/body/eval_jaxpr/reduce_scatter | solution.py:195
  875.0 9.8 copy-start.44
  889.1 71.6 %all-gather.24.cloned.1.call-start = ((), (), s32[]{:S(2)}) async-start(), calls=%async_computation.23 | async-start | bytes 2621440 | tf_op jit(solution)/shard_map/while/body/eval_jaxpr/all_gather | solution.py:202
  937.9 94.2 %reduce-scatter.28.cloned.1.call-start = ((), (), s32[]{:S(2)}) async-start(), calls=%async_computation.24 | async-start | bytes 2621440 | tf_op jit(solution)/shard_map/while/body/eval_jaxpr/reduce_scatter | solution.py:228
  1002.1 8.3 copy-start.41
  1002.4 8.0 copy-start.43
  1002.4 8.0 copy-start.47
  1010.4 6.9 copy-start.12
  1010.4 9.4 copy-start.23
  1010.4 9.4 copy-start.7
  1010.4 9.4 copy-start.11
  1019.8 8.8 copy-start.24
  1023.0 9.2 copy-start.6
  1023.0 11.4 copy-start.22
  1037.5 25.1 %reduce-scatter.20.cloned.1.call-start = ((), (), s32[]{:S(2)}) async-start(), calls=%async_computation.13 | async-start | bytes 655360
  1039.3 90.5 %reduce-scatter.14.cloned.1.call-start = ((), (), s32[]{:S(2)}) async-start(), calls=%async_computation.10 | async-start | bytes 1179648 | tf_op jit(solution)/shard_map/reduce_scatter | solution.py:282
  1039.9 167.1 %reduce-scatter.12.cloned.1.call-start = ((), (), s32[]{:S(2)}) async-start(), calls=%async_computation.9 | async-start | bytes 3538944 | tf_op jit(solution)/shard_map/reduce_scatter | solution.py:281
  1040.5 257.0 %reduce-scatter.16.cloned.1.call-start = ((), (), s32[]{:S(2)}) async-start(), calls=%async_computation.11 | async-start | bytes 4718592 | tf_op jit(solution)/shard_map/reduce_scatter | solution.py:283
  1040.5 351.1 %copy-start.25 = (f32[12,1024]{1,0:T(8,128)S(1)}, f32[12,1024]{1,0:T(8,128)}, u32[]{:S(2)}) copy-start(f32[12,1024]{1,0:T(8,128)} %get-tuple-element.466) | copy-start | bytes 147460
  1040.6 394.1 %copy-start.31 = (f32[12,1024]{1,0:T(8,128)S(1)}, f32[12,1024]{1,0:T(8,128)}, u32[]{:S(2)}) copy-start(f32[12,1024]{1,0:T(8,128)} %get-tuple-element.1283) | copy-start | bytes 147460
  1040.6 394.1 %copy-start.39 = (f32[12,1024]{1,0:T(8,128)S(1)}, f32[12,1024]{1,0:T(8,128)}, u32[]{:S(2)}) copy-start(f32[12,1024]{1,0:T(8,128)} %param.44) | copy-start | bytes 147460
  1041.2 395.2 %copy-start.32 = (f32[128,256]{1,0:T(8,128)S(1)}, f32[128,256]{1,0:T(8,128)}, u32[]{:S(2)}) copy-start(f32[128,256]{1,0:T(8,128)} %param.32) | copy-start | bytes 393220
  1041.2 395.2 %copy-start.38 = (f32[128,256]{1,0:T(8,128)S(1)}, f32[128,256]{1,0:T(8,128)}, u32[]{:S(2)}) copy-start(f32[128,256]{1,0:T(8,128)} %param.38) | copy-start | bytes 393220
  1041.3 396.9 %copy-start.30 = (f32[128,3,256]{2,0,1:T(8,128)S(1)}, f32[128,3,256]{2,0,1:T(8,128)}, u32[]{:S(2)}) copy-start(f32[128,3,256]{2,0,1:T(8,128)} %param.31) | copy-start | bytes 1179652
  1041.3 347.9 %reduce-scatter.18.cloned.1.call-start = ((), (), s32[]{:S(2)}) async-start(), calls=%async_computation.12 | async-start | bytes 4718592 | tf_op jit(solution)/shard_map/reduce_scatter | solution.py:284
  1041.3 399.3 %copy-start.26 = (f32[128,1024]{1,0:T(8,128)S(1)}, f32[128,1024]{1,0:T(8,128)}, u32[]{:S(2)}) copy-start(f32[128,1024]{1,0:T(8,128)} %param.34) | copy-start | bytes 1572868
  1041.3 399.3 %copy-start.33 = (f32[128,1024]{1,0:T(8,128)S(1)}, f32[128,1024]{1,0:T(8,128)}, u32[]{:S(2)}) copy-start(f32[128,1024]{1,0:T(8,128)} %param.42) | copy-start | bytes 1572868
  1299.9 142.1 %copy-start.27 = (f32[128,1024]{1,0:T(8,128)S(1)}, f32[128,1024]{1,0:T(8,128)}, u32[]{:S(2)}) copy-start(f32[128,1024]{1,0:T(8,128)} %param.33) | copy-start | bytes 1572868
  1299.9 142.1 %copy-start.28 = (f32[128,1024]{1,0:T(8,128)S(1)}, f32[128,1024]{1,0:T(8,128)}, u32[]{:S(2)}) copy-start(f32[128,1024]{1,0:T(8,128)} %reduce-scatter.16.cloned.1.call-done) | copy-start | bytes 1572868
  1389.1 51.5 %copy-start.29 = (f32[128,1024]{1,0:T(8,128)S(1)}, f32[128,1024]{1,0:T(8,128)}, u32[]{:S(2)}) copy-start(f32[128,1024]{1,0:T(8,128)} %reduce-scatter.18.cloned.1.call-done) | copy-start | bytes 1572868
  1434.7 7.3 copy-start.35
  1434.7 7.3 copy-start.36
  (57 other events, 148.6 us)
Sparse Core Ops, SparseCore 0:
  19.9 49.7 all-gather.13
  71.8 21.2 all-gather.11
  118.6 44.4 reduce-scatter.21
  165.9 49.2 all-gather.17
  217.3 21.0 all-gather.15
  241.2 49.2 all-gather.19
  297.2 42.9 reduce-scatter.23
  344.6 22.5 all-gather.21
  381.4 44.5 reduce-scatter.25
  430.3 22.5 all-gather.23
  492.9 31.4 reduce-scatter.27
  530.1 47.2 all-gather.13
  579.6 21.2 all-gather.11
  626.4 44.4 reduce-scatter.21
  673.7 49.2 all-gather.17
  725.1 21.0 all-gather.15
  749.0 49.2 all-gather.19
  805.0 42.9 reduce-scatter.23
  852.3 22.5 all-gather.21
  889.2 44.4 reduce-scatter.25
  938.0 22.5 all-gather.23
  1000.7 31.4 reduce-scatter.27
Sparse Core Ops, SparseCore 1:
  1041.1 21.5 reduce-scatter.19
  1066.3 63.5 reduce-scatter.13
  1133.3 73.6 reduce-scatter.11
  1210.6 86.8 reduce-scatter.15
  1301.6 87.5 reduce-scatter.17
where the time goes:
time: 1460 us; the launch traced here: 1450 us
  waiting for transfers between devices  999 us (68%)
  matrix products  188 us (13%)
  blocking collectives  111 us (8%)
  other arithmetic  64 us (4%)
  local copies, waits for them, and re-layouts  61.4 us (4%)
  between operations  21.2 us (1%)
    all_gather x2, waiting for transfers between devices, one_document(): lax.all_gather(shards[2], 'dp', axis=0, tiled=True)  96.6 us
    reduce_scatter x2, waiting for transfers between devices, one_document(): lax.psum_scatter(lax.dot_general(part_rows, full_one, contract_last, pref...  89.2 us
    reduce_scatter x1, waiting for transfers between devices, local(): lax.psum_scatter(sum_two, 'dp', scatter_dimension=0, tiled=True)  89.2 us
    reduce_scatter x1, waiting for transfers between devices, local(): lax.psum_scatter(sum_one, 'dp', scatter_dimension=0, tiled=True)  87.5 us
    reduce_scatter x2, waiting for transfers between devices, one_document(): lax.psum_scatter(lax.dot_general(part_rows, full_two, contract_last, pref...  86.2 us
    reduce_scatter x2, waiting for transfers between devices, one_document(): lax.psum_scatter(lax.dot_general(part_rows, full_out, contract_last, pref...  84.8 us
    reduce_scatter x1, waiting for transfers between devices, local(): lax.psum_scatter(sum_qkv, 'dp', scatter_dimension=0, tiled=True)  75.6 us
    all_gather x2, waiting for transfers between devices, one_document(): lax.all_gather(shards[3], 'dp', axis=0, tiled=True)  74.4 us
  transfers between devices with their start and end apart: 27, of which 27 were waited for; matrix products, arithmetic and copies ran while one was open for 7% of the time, Pallas kernels for 0%

commit v1 on v0

v1 whole, which is shorter than its diff:
```python
from functools import partial
import math

import jax
import jax.numpy as jnp
from jax import lax
from jax.experimental import pallas as pl
from jax.experimental.pallas import tpu as pltpu
from jax.sharding import PartitionSpec as P

D = 1024
HD = 64
FF = 4096
DOC_LEN = 1024
CLS_GAP = 256
STEP = 10

MESH = pl.DeviceIdType.MESH
ANY = pl.BlockSpec(memory_space=pl.ANY)
VMEM = pl.BlockSpec(memory_space=pltpu.VMEM)
DMA = pltpu.SemaphoreType.DMA
f32 = jnp.float32
bf16 = jnp.bfloat16

norm_eps = 1e-05
beta_one = 0.9
beta_two = 0.999
adam_eps = 1e-08
weight_decay = 0.01
vector_rate = 0.4
highest = lax.Precision.HIGHEST
contract_last = (((1,), (1,)), ((), ()))
contract_first = (((0,), (0,)), ((), ()))


def layer_norm(values_in, scale_vec, shift_vec):
    row_mean = jnp.mean(values_in, axis=-1, keepdims=True)
    centered = values_in - row_mean
    row_var = jnp.mean(centered * centered, axis=-1, keepdims=True)
    return centered * lax.rsqrt(row_var + norm_eps) * scale_vec + shift_vec


def clip_limit(params_all, tokens_all):
    return 0.005 * math.sqrt(params_all * tokens_all)


def matrix_rates(model_width, hidden, length):
    out_fan = max(1, 3 * model_width // length)
    return (
        1.5 / math.sqrt(model_width),
        1.5 / math.sqrt(out_fan),
        1.5 / math.sqrt(model_width),
        1.5 / math.sqrt(hidden),
    )


def adam_update(parameter, gradient, first_old, second_old, step_rate, decay_rate):
    first_new = beta_one * first_old + (1.0 - beta_one) * gradient
    second_new = beta_two * second_old + (1.0 - beta_two) * gradient * gradient
    first_hat = first_new / (1.0 - beta_one**STEP)
    second_hat = second_new / (1.0 - beta_two**STEP)
    updated = parameter - step_rate * (
        first_hat / (jnp.sqrt(second_hat) + adam_eps) + decay_rate * parameter
    )
    return (updated, first_new, second_new)


class Place:
    def __init__(self):
        dp, mp = lax.axis_index("dp"), lax.axis_index("mp")
        self.z, self.x = dp // 2, dp % 2
        self.y, self.k = mp // 2, mp % 2

    def near(self, axis):
        z, x, y, k = self.z, self.x, self.y, self.k
        if axis == "x":
            x = 1 - x
        elif axis == "y":
            y = 1 - y
        else:
            k = 1 - k
        return (z * 2 + x, y * 2 + k)

    def along(self, j, nz):
        return ((self.z + j) % nz * 2 + self.x, self.y * 2 + self.k)


def greet(place, nz, axes="xyk"):
    barrier = pltpu.get_barrier_semaphore()
    for axis in axes:
        pl.semaphore_signal(barrier, inc=1, device_id=place.near(axis), device_id_type=MESH)
    if nz > 1:

        def one(j, carry):
            pl.semaphore_signal(barrier, inc=1, device_id=place.along(j, nz), device_id_type=MESH)
            return carry

        lax.fori_loop(1, nz, one, 0)
    pl.semaphore_wait(barrier, len(axes) + nz - 1)


def remote(src, dst, send, recv, where):
    return pltpu.make_async_remote_copy(
        src_ref=src, dst_ref=dst, send_sem=send, recv_sem=recv, device_id=where, device_id_type=MESH
    )


def each(start, stop, body):
    def one(j, carry):
        body(j)
        return carry

    lax.fori_loop(start, stop, one, 0)


class Gather:
    def __init__(self, place, own, full, c0, cols, sems, c):
        self.p, self.own, self.full = place, own, full
        self.nz = full.shape[1]
        half = cols // 2
        self.all, self.a, self.b = pl.ds(c0, cols), pl.ds(c0, half), pl.ds(c0 + half, half)
        self.sems, self.c = sems, c

    def piece(self, y, z, x, cols):
        return self.full.at[y, z, x, :, cols]

    def sem(self, kind, j):
        return self.sems.at[0, kind, self.c, j], self.sems.at[1, kind, self.c, j]

    def to(self, kind, j, src, dst, where):
        return remote(src, dst, *self.sem(kind, j), where)

    def along_z(self, j):
        p = self.p
        return self.to(
            0, j, self.own.at[:, self.all], self.piece(p.y, p.z, p.x, self.all), p.along(j, self.nz)
        )

    def own_xy(self, kind):
        p = self.p
        return self.to(
            kind,
            0,
            self.own.at[:, self.all],
            self.piece(p.y, p.z, p.x, self.all),
            p.near("x" if kind == 1 else "y"),
        )

    def pass_xy(self, kind, j):
        p = self.p
        ref = self.piece(p.y, (p.z + self.nz - j) % self.nz, p.x, self.all)
        return self.to(kind, j, ref, ref, p.near("x" if kind == 1 else "y"))

    def pass_half(self, kind, j):
        p = self.p
        z = (p.z + self.nz - j) % self.nz
        if kind == 3:
            ref = self.piece(p.y, z, 1 - p.x, self.a)
            return self.to(3, j, ref, ref, p.near("y"))
        ref = self.piece(1 - p.y, z, p.x, self.b)
        return self.to(4, j, ref, ref, p.near("x"))

    def stage(self, s):
        nz = self.nz
        if s == 0:
            each(1, nz, lambda j: self.along_z(j).start())
            self.own_xy(1).start()
            self.own_xy(2).start()
        elif s == 1:

            def one(j):
                self.along_z(j).wait()
                self.pass_xy(1, j).start()
                self.pass_xy(2, j).start()

            each(1, nz, one)
        elif s == 2:

            def first(kind):
                self.own_xy(kind).wait()
                self.pass_half(kind + 2, 0).start()

            first(1)
            first(2)

            def two(j):
                for kind in (1, 2):
                    self.pass_xy(kind, j).wait()
                    self.pass_half(kind + 2, j).start()

            each(1, nz, two)
        else:

            def three(j):
                self.pass_half(3, j).wait()
                self.pass_half(4, j).wait()

            each(0, nz, three)


def pump(chunks, stages, t):
    for s in reversed(range(stages)):
        if 0 <= t - s < len(chunks):
            chunks[t - s].stage(s)


def gather_kernel(
    x_ref, cot_ref, wq, wo, w1, w2, x_all, cot_half, gq, go, g1, g2, sems, side, local_sem
):
    p = Place()
    nz = gq.shape[1]
    greet(p, nz)
    swap_x = remote(x_ref.at[1 - p.y], x_all.at[p.y, p.k], side.at[0, 0], side.at[1, 0], p.near("y"))
    swap_x.start()
    keep_x = pltpu.make_async_copy(x_ref.at[p.y], x_all.at[p.y, p.k], local_sem.at[0])
    keep_x.start()
    give_x = remote(x_ref.at[p.y], x_all.at[p.y, p.k], side.at[0, 1], side.at[1, 1], p.near("k"))
    give_x.start()
    keeps = []
    for i, (own, full) in enumerate(((wq, gq), (wo, go), (w1, g1), (w2, g2))):
        keeps.append(
            pltpu.make_async_copy(own, full.at[p.y, p.z, p.x], local_sem.at[1 + i])
        )
        keeps[-1].start()
    chunks = []
    for own, full, width in ((wq, gq, 768), (wo, go, 256), (w1, g1, 512), (w2, g2, 512)):
        for c0 in range(0, own.shape[1], width):
            chunks.append(Gather(p, own, full, c0, width, sems, len(chunks)))
    swap_cot = remote(cot_ref, cot_half, side.at[0, 2], side.at[1, 2], p.near("y"))
    for t in range(len(chunks) + 3):
        pump(chunks, 4, t)
        if t == 1:
            swap_x.wait()
            ref = x_all.at[1 - p.y, p.k]
            pass_x = remote(ref, ref, side.at[0, 3], side.at[1, 3], p.near("k"))
            pass_x.start()
            swap_cot.start()
    keep_x.wait()
    give_x.wait()
    pass_x.wait()
    swap_cot.wait()
    for keep in keeps:
        keep.wait()


def gather_all(x_loc, cot_send, shards):
    nz = lax.axis_size("dp") // 2
    rows = shards[0].shape[0]
    shapes = [
        jax.ShapeDtypeStruct((2, 2) + x_loc.shape[1:], bf16),
        jax.ShapeDtypeStruct(cot_send.shape, bf16),
    ] + [jax.ShapeDtypeStruct((2, nz, 2, rows, s.shape[1]), bf16) for s in shards]
    n_chunks = 6
    return pl.pallas_call(
        gather_kernel,
        out_shape=shapes,
        in_specs=[ANY] * 6,
        out_specs=[ANY] * 6,
        scratch_shapes=[
            DMA((2, 5, n_chunks, nz)),
            DMA((2, 4)),
            DMA((5,)),
        ],
        compiler_params=pltpu.CompilerParams(collective_id=0, has_side_effects=True),
        name="gather_weights",
    )(x_loc, cot_send, *shards)


class Reduce:
    def __init__(self, place, part, total, buffers, c0, cols, sems, c):
        self.p, self.part, self.total = place, part, total
        self.ra, self.rb, self.rx, self.ry, self.rz = buffers
        self.nz = part.shape[1]
        self.half = cols // 2
        self.all, self.a, self.b = pl.ds(c0, cols), pl.ds(c0, self.half), pl.ds(c0 + self.half, self.half)
        self.in_a = pl.ds(c0 // 2, self.half)
        self.sems, self.c = sems, c

    def to(self, kind, j, src, dst, where):
        return remote(src, dst, self.sems.at[0, kind, self.c, j], self.sems.at[1, kind, self.c, j], where)

    def send_half(self, kind, z):
        p = self.p
        if kind == 0:
            return self.to(
                0, z, self.part.at[1 - p.y, z, 1 - p.x, :, self.a], self.ra.at[z, :, self.in_a], p.near("y")
            )
        return self.to(
            1, z, self.part.at[1 - p.y, z, 1 - p.x, :, self.b], self.rb.at[z, :, self.in_a], p.near("x")
        )

    def send_sum(self, kind, z):
        p = self.p
        if kind == 2:
            return self.to(2, z, self.ra.at[z, :, self.in_a], self.rx.at[z, :, self.a], p.near("x"))
        return self.to(3, z, self.rb.at[z, :, self.in_a], self.ry.at[z, :, self.b], p.near("y"))

    def send_own(self, kind, z):
        p = self.p
        if kind == 5:
            return self.to(
                5, z, self.part.at[p.y, z, 1 - p.x, :, self.b], self.rx.at[z, :, self.b], p.near("x")
            )
        return self.to(
            6, z, self.part.at[1 - p.y, z, p.x, :, self.a], self.ry.at[z, :, self.a], p.near("y")
        )

    def send_z(self, j):
        p = self.p
        z = (p.z + j) % self.nz
        return self.to(4, j, self.rx.at[z, :, self.all], self.rz.at[j, :, self.all], p.along(j, self.nz))

    def stage(self, s):
        p, nz = self.p, self.nz
        if s == 0:

            def zero(z):
                self.send_half(0, z).start()
                self.send_half(1, z).start()

            each(0, nz, zero)
        elif s == 1:

            def one(z):
                self.send_half(0, z).wait()
                into = self.ra.at[z, :, self.in_a]
                into[...] = (
                    into[...].astype(f32) + self.part[p.y, z, 1 - p.x, :, self.a].astype(f32)
                ).astype(bf16)
                self.send_sum(2, z).start()
                self.send_own(5, z).start()
                self.send_half(1, z).wait()
                into = self.rb.at[z, :, self.in_a]
                into[...] = (
                    into[...].astype(f32) + self.part[1 - p.y, z, p.x, :, self.b].astype(f32)
                ).astype(bf16)
                self.send_sum(3, z).start()
                self.send_own(6, z).start()

            each(0, nz, one)
        elif s == 2:

            def add(z):
                self.send_sum(2, z).wait()
                self.send_own(5, z).wait()
                self.send_sum(3, z).wait()
                self.send_own(6, z).wait()
                return (
                    self.part[p.y, z, p.x, :, self.all].astype(f32)
                    + self.rx[z, :, self.all].astype(f32)
                    + self.ry[z, :, self.all].astype(f32)
                )

            def two(j):
                z = (p.z + j) % nz
                self.rx[z, :, self.all] = add(z).astype(bf16)
                self.send_z(j).start()

            each(1, nz, two)
            self.total[:, self.all] = add(p.z)
        else:

            def three(j):
                self.send_z(j).wait()
                self.total[:, self.all] += self.rz[j, :, self.all].astype(f32)

            each(1, nz, three)


def reduce_kernel(widths, *refs):
    n = len(widths)
    parts, totals = refs[:n], refs[n : 2 * n]
    buffers = [refs[2 * n + 5 * i : 2 * n + 5 * i + 5] for i in range(n)]
    (sems,) = refs[7 * n :]
    p = Place()
    greet(p, parts[0].shape[1], "xy")
    chunks = []
    for i, width in enumerate(widths):
        for c0 in range(0, parts[i].shape[-1], width):
            chunks.append(Reduce(p, parts[i], totals[i], buffers[i], c0, width, sems, len(chunks)))
    for t in range(len(chunks) + 3):
        pump(chunks, 4, t)


def reduce_all(parts, widths):
    nz, rows = parts[0].shape[1], parts[0].shape[3]
    scratch = []
    for part in parts:
        cols = part.shape[-1]
        scratch += [pltpu.VMEM((nz, rows, cols // 2), bf16)] * 2
        scratch += [pltpu.VMEM((nz, rows, cols), bf16)] * 3
    n_chunks = sum(part.shape[-1] // width for part, width in zip(parts, widths))
    return pl.pallas_call(
        partial(reduce_kernel, widths),
        out_shape=[jax.ShapeDtypeStruct((rows, part.shape[-1]), f32) for part in parts],
        in_specs=[VMEM] * len(parts),
        out_specs=[VMEM] * len(parts),
        scratch_shapes=scratch + [DMA((2, 7, n_chunks, nz))],
        compiler_params=pltpu.CompilerParams(
            collective_id=1, has_side_effects=True, vmem_limit_bytes=56 * 2**20
        ),
        name="reduce_gradients",
    )(*parts)


def swap_kernel(axis, src, dst, sems):
    p = Place()
    greet(p, 1, axis)
    copy = remote(src, dst, sems.at[0], sems.at[1], p.near(axis))
    copy.start()
    copy.wait()


def swap(array, axis, call):
    return pl.pallas_call(
        partial(swap_kernel, axis),
        out_shape=jax.ShapeDtypeStruct(array.shape, array.dtype),
        in_specs=[VMEM],
        out_specs=VMEM,
        scratch_shapes=[DMA((2,))],
        compiler_params=pltpu.CompilerParams(
            collective_id=call, has_side_effects=True, vmem_limit_bytes=32 * 2**20
        ),
        name="swap_" + axis,
    )(array)


def heads_of(columns):
    return columns.reshape(columns.shape[0], -1, HD)


def attend_forward(key_heads, value_heads, query_block):
    scores = jnp.einsum(
        "qhd,khd->hqk", query_block, key_heads, preferred_element_type=jnp.float32
    ) * HD ** (-0.5)
    row_top = jnp.max(scores, axis=-1, keepdims=True)
    raised = jnp.exp(scores - row_top)
    row_total = jnp.sum(raised, axis=-1, keepdims=True)
    shares = (raised / row_total).astype(jnp.bfloat16)
    mixed = jnp.einsum("hqk,khd->qhd", shares, value_heads, preferred_element_type=jnp.float32)
    return (mixed.astype(jnp.bfloat16), (row_top + jnp.log(row_total))[..., 0])


def attend_backward(key_heads, value_heads, carry, block):
    query_block, log_block, grad_block = block
    key_sum, value_sum = carry
    scores = jnp.einsum(
        "qhd,khd->hqk", query_block, key_heads, preferred_element_type=jnp.float32
    ) * HD ** (-0.5)
    shares = jnp.exp(scores - log_block[..., None])
    value_sum = value_sum + jnp.einsum(
        "hqk,qhd->khd", shares.astype(jnp.bfloat16), grad_block, preferred_element_type=jnp.float32
    )
    dshares = jnp.einsum(
        "qhd,khd->hqk", grad_block, value_heads, preferred_element_type=jnp.float32
    )
    dscores = (shares * (dshares - jnp.sum(shares * dshares, axis=-1, keepdims=True))).astype(
        jnp.bfloat16
    )
    query_grad = jnp.einsum(
        "hqk,khd->qhd", dscores, key_heads, preferred_element_type=jnp.float32
    ) * HD ** (-0.5)
    key_sum = key_sum + jnp.einsum(
        "hqk,qhd->khd", dscores, query_block, preferred_element_type=jnp.float32
    ) * HD ** (-0.5)
    return ((key_sum, value_sum), query_grad)


def dot(a, b, dims=(((1,), (0,)), ((), ()))):
    return lax.dot_general(a, b, dims, preferred_element_type=f32)


def local(
    tokens, out_cot, cls_offset, w_qkv, w_out, w_one, w_two, vectors,
    m_qkv, v_qkv, m_out, v_out, m_one, v_one, m_two, v_two, m_vec, v_vec,
):
    rows_dev = tokens.shape[1]
    mp_rank = lax.axis_index("mp")
    y, k = mp_rank // 2, mp_rank % 2
    length = rows_dev * lax.axis_size("mp")
    rows_w = w_qkv.shape[0]
    head_cols = w_qkv.shape[2]
    ff_cols = w_one.shape[1]

    def mine(row, width):
        return [
            lax.dynamic_slice_in_dim(row, (2 * b + k) * width, width) for b in range(2)
        ]

    query_bias = mine(vectors[0], head_cols)
    value_bias = mine(vectors[1], head_cols)
    ff_bias = mine(vectors[8:].reshape(-1), ff_cols)
    shards = (
        w_qkv.astype(bf16).reshape(rows_w, 3 * head_cols),
        w_out.astype(bf16),
        w_one.astype(bf16),
        w_two.astype(bf16),
    )
    cot_own = lax.dynamic_index_in_dim(out_cot, y, 0, keepdims=False)
    cot_send = lax.dynamic_index_in_dim(out_cot, 1 - y, 0, keepdims=False).astype(bf16)
    x_all, cot_other, *full = gather_all(tokens, cot_send, shards)
    full_qkv, full_out, full_one, full_two = [g.reshape(2, D, g.shape[-1]) for g in full]
    x_doc = x_all.reshape(length, D)

    def own_rows(a):
        return lax.dynamic_index_in_dim(a.reshape(2, 2, rows_dev, D), k, 1, keepdims=False)

    def other_rows(a):
        return lax.dynamic_index_in_dim(a.reshape(2, 2, rows_dev, D), 1 - k, 1, keepdims=False)

    def by_y(own, other):
        return jnp.where(y == 0, jnp.stack([own, other]), jnp.stack([other, own]))

    def core_sum(partial_sum, call):
        got = swap(other_rows(partial_sum).astype(bf16), "k", call)
        return own_rows(partial_sum) + got.astype(f32)

    def core_gather(rows, call):
        got = swap(rows, "k", call)
        pair = jnp.where(k == 0, jnp.stack([rows, got], 1), jnp.stack([got, rows], 1))
        return pair.reshape(length, D)

    cot = by_y(cot_own, cot_other.astype(f32))
    x_rows = own_rows(x_doc).astype(f32)

    queries, keys_all, values_all = [], [], []
    for b in range(2):
        projected = dot(x_doc, full_qkv[b])
        queries.append((projected[:, :head_cols] + query_bias[b]).astype(bf16))
        keys_all.append(projected[:, head_cols : 2 * head_cols].astype(bf16))
        values_all.append((projected[:, 2 * head_cols :] + value_bias[b]).astype(bf16))
    queries, keys_all, values_all = [jnp.concatenate(a, 1) for a in (queries, keys_all, values_all)]
    key_heads, value_heads = heads_of(keys_all), heads_of(values_all)
    query_blocks = heads_of(queries).reshape(2, length // 2, -1, HD)
    attended, log_sums = lax.map(partial(attend_forward, key_heads, value_heads), query_blocks)
    attended = attended.reshape(length, 2 * head_cols)
    part_out = sum(
        dot(attended[:, b * head_cols : (b + 1) * head_cols], full_out[b], contract_last)
        for b in range(2)
    )
    z_one = x_rows + core_sum(part_out, 2) + vectors[2]
    y_one, first_back = jax.vjp(layer_norm, z_one, vectors[3], vectors[4])
    normed_all = core_gather(y_one.astype(bf16), 3)
    pre_act = [dot(normed_all, full_one[b]) + ff_bias[b] for b in range(2)]
    hidden = [jax.nn.gelu(u, approximate=False).astype(bf16) for u in pre_act]
    part_two = sum(dot(hidden[b], full_two[b], contract_last) for b in range(2))
    z_two = y_one + core_sum(part_two, 4) + vectors[5]
    layer_out, second_back = jax.vjp(layer_norm, z_two, vectors[6], vectors[7])
    offsets = lax.dynamic_index_in_dim(cls_offset, y, 0, keepdims=False)
    positions = offsets + jnp.arange(offsets.shape[0], dtype=jnp.int32) * CLS_GAP
    row_ids = (
        (2 * jnp.arange(2, dtype=jnp.int32)[:, None] + k) * rows_dev
        + jnp.arange(rows_dev, dtype=jnp.int32)[None, :]
    )
    picks = (
        jnp.sum((positions[:, None, None] == row_ids[None]).astype(f32), axis=0)
        / offsets.shape[0]
    )
    pool_part = jnp.einsum("br,brd->d", picks, layer_out, precision=highest)
    pool_parts = jnp.where(jnp.arange(2)[:, None] == y, pool_part[None], 0.0)
    dz_two, dscale_two, dshift_two = second_back(cot)
    dffn_all = core_gather(dz_two.astype(bf16), 5)
    grad_two = [dot(dffn_all, hidden[b], contract_first) for b in range(2)]
    dpre = []
    for b in range(2):
        dhidden = dot(dffn_all, full_two[b])
        gelu_back = jax.vjp(partial(jax.nn.gelu, approximate=False), pre_act[b])[1]
        dpre.append(gelu_back(dhidden)[0].astype(bf16))
    grad_one = [dot(normed_all, dpre[b], contract_first) for b in range(2)]
    dff_bias = [jnp.sum(d, axis=0, dtype=f32) for d in dpre]
    part_one = sum(dot(dpre[b], full_one[b], contract_last) for b in range(2))
    dz_one, dscale_one, dshift_one = first_back(dz_two + core_sum(part_one, 6))
    dbranch_all = core_gather(dz_one.astype(bf16), 7)
    grad_out = [
        dot(dbranch_all, attended[:, b * head_cols : (b + 1) * head_cols], contract_first)
        for b in range(2)
    ]
    dattended = jnp.concatenate([dot(dbranch_all, full_out[b]).astype(bf16) for b in range(2)], 1)
    grad_blocks = heads_of(dattended).reshape(2, length // 2, -1, HD)
    zero_heads = jnp.zeros(key_heads.shape, f32)
    (key_sum, value_sum), query_grad = lax.scan(
        partial(attend_backward, key_heads, value_heads),
        (zero_heads, zero_heads),
        (query_blocks, log_sums, grad_blocks),
    )
    dparts = [
        a.reshape(length, 2, head_cols).astype(bf16) for a in (query_grad, key_sum, value_sum)
    ]
    dprojected = [jnp.concatenate([a[:, b] for a in dparts], 1) for b in range(2)]
    grad_qkv = [dot(x_doc, dprojected[b], contract_first) for b in range(2)]
    part_x = sum(dot(dprojected[b], full_qkv[b], contract_last) for b in range(2))
    input_rows = dz_one + core_sum(part_x, 8)
    back = swap(
        lax.dynamic_index_in_dim(input_rows, 1 - y, 0, keepdims=False).astype(bf16), "y", 9
    )
    input_grad = by_y(
        lax.dynamic_index_in_dim(input_rows, y, 0, keepdims=False), back.astype(f32)
    )

    def spread(width, blocks):
        row = jnp.zeros((4 * width,), f32)
        for b in range(2):
            row = lax.dynamic_update_slice(row, blocks[b], ((2 * b + k) * width,))
        return row

    head_sums = [jnp.sum(d, axis=0, dtype=f32) for d in dprojected]
    vec_local = jnp.concatenate(
        [
            jnp.stack(
                [
                    spread(head_cols, [h[:head_cols] for h in head_sums]),
                    spread(head_cols, [h[2 * head_cols :] for h in head_sums]),
                    jnp.sum(dz_one, axis=(0, 1)),
                    dscale_one,
                    dshift_one,
                    jnp.sum(dz_two, axis=(0, 1)),
                    dscale_two,
                    dshift_two,
                ]
            ),
            spread(ff_cols, dff_bias).reshape(-1, D),
        ]
    )
    pooled = lax.psum_scatter(pool_parts, "mp", scatter_dimension=1, tiled=True)

    def as_parts(blocks):
        return jnp.stack([b.astype(bf16) for b in blocks]).reshape(
            2, D // rows_w // 2, 2, rows_w, -1
        )

    g_two, g_one, g_out, g_qkv = reduce_all(
        [as_parts(grad_two), as_parts(grad_one), as_parts(grad_out), as_parts(grad_qkv)],
        (512, 512, 256, 768),
    )
    g_qkv = g_qkv.reshape(w_qkv.shape)
    own_squares = (
        jnp.sum(g_qkv * g_qkv)
        + jnp.sum(g_out * g_out)
        + jnp.sum(g_one * g_one)
        + jnp.sum(g_two * g_two)
    )
    g_vec, squares_all = lax.psum((vec_local, own_squares), ("dp", "mp"))
    grad_norm = jnp.sqrt(squares_all + jnp.sum(g_vec * g_vec))
    tokens_all = tokens.shape[0] * length * lax.axis_size("dp")
    factor = jnp.minimum(1.0, clip_limit(4 * D * D + 2 * D * FF, tokens_all) / (grad_norm + 1e-06))
    rates = matrix_rates(D, FF, DOC_LEN)
    return (
        pooled,
        input_grad,
        grad_norm,
        *adam_update(w_qkv, g_qkv * factor, m_qkv, v_qkv, rates[0], weight_decay),
        *adam_update(w_out, g_out * factor, m_out, v_out, rates[1], weight_decay),
        *adam_update(w_one, g_one * factor, m_one, v_one, rates[2], weight_decay),
        *adam_update(w_two, g_two * factor, m_two, v_two, rates[3], weight_decay),
        *adam_update(vectors, g_vec * factor, m_vec, v_vec, vector_rate, 0.0),
    )


def solution(mesh):
    rows, wide, flat, whole = P("dp", "mp", None), P("dp", None, "mp"), P("dp", "mp"), P()
    return jax.shard_map(
        local,
        mesh=mesh,
        in_specs=(rows, rows, P("dp", None), wide, flat, flat, flat, whole)
        + (wide, wide)
        + (flat,) * 6
        + (whole, whole),
        out_specs=(flat, rows, whole) + (wide,) * 3 + (flat,) * 9 + (whole,) * 3,
        check_vma=False,
    )
```

time: 1460 us -> 672 us (0.46)
  waiting for transfers between devices: 999 us -> 0.02 us
  Pallas kernels: 0 us -> 289 us
  blocking collectives: 111 us -> 42.5 us
  matrix products: 188 us -> 157 us
  other arithmetic: 64 us -> 89.5 us
    reduce_scatter x12 -> x0, waiting for transfers between devices: 592 us -> none  [the longest x2 89.2 us: one_document(): lax.psum_scatter(lax.dot_general(part_rows, full_one, contract_last, pref...]
    all_gather x14 -> x0, waiting for transfers between devices: 380 us -> none  [the longest x2 96.6 us: one_document(): lax.all_gather(shards[2], 'dp', axis=0, tiled=True)]
    pallas_call x0 -> x10, Pallas kernels: none -> 289 us  [the longest x1 133 us: gather_all(): pl.pallas_call(gather_kernel, out_shape=shapes, in_specs=[ANY] * 6, out_s...]
    all_gather x2 -> x0, blocking collectives: 70.1 us -> none  [one_document(): lax.all_gather(shards[1], 'dp', axis=0, tiled=True)]
    dot_general x26 -> x25, matrix products: 140 us -> 89.7 us  [the longest x24 88.3 us: dot(): return lax.dot_general(a, b, dims, preferred_element_type=f32)]
    unnamed x6 -> x2, waiting for transfers between devices: 23 us -> 0.02 us
    unnamed x33 -> x196, local copies, waits for them, and re-layouts: 5.93 us -> 26.6 us
    reshape x10 -> x2, local copies, waits for them, and re-layouts: 15.7 us -> 0.84 us  [the longest x1 0.83 us: local(): w_qkv.astype(bf16).reshape(rows_w, 3 * head_cols)]
  transfers between devices with their start and end apart: 27 -> 1, of which waited for: 27 -> 0; matrix products, arithmetic and copies ran while one was open for 7% -> 27% of each run, Pallas kernels for 0% -> 22%
where the time goes in v1:
time: 672 us; the launch traced here: 662 us
  Pallas kernels  289 us (43%)
  matrix products  157 us (23%)
  other arithmetic  89.5 us (13%)
  local copies, waits for them, and re-layouts  62.6 us (9%)
  blocking collectives  42.5 us (6%)
  between operations  21 us (3%)
    pallas_call x1, Pallas kernels, gather_all(): pl.pallas_call(gather_kernel, out_shape=shapes, in_specs=[ANY] * 6, out_s...  133 us
    pallas_call x1, Pallas kernels, reduce_all(): pl.pallas_call(partial(reduce_kernel, widths), out_shape=[jax.ShapeDtypeS...  124 us
    dot_general x24, matrix products, dot(): return lax.dot_general(a, b, dims, preferred_element_type=f32)  88.3 us
    psum x1, blocking collectives, local(): g_vec, squares_all = lax.psum((vec_local, own_squares), ('dp', 'mp'))  42.5 us
    pallas_call x8, Pallas kernels, swap(): pl.pallas_call(partial(swap_kernel, axis), out_shape=jax.ShapeDtypeStruct...  31.8 us
    unnamed x196, local copies, waits for them, and re-layouts  26.6 us
    convert_element_type x2, other arithmetic, attend_backward(): (shares * (dshares - jnp.sum(shares * dshares, axis=-1, keepdims=True)))....  20.9 us
    dot_general x2, matrix products, attend_backward(): jnp.einsum('qhd,khd->hqk', grad_block, value_heads, preferred_element_typ...  19.2 us
  transfers between devices with their start and end apart: 1, of which 0 were waited for; matrix products, arithmetic and copies ran while one was open for 27% of the time, Pallas kernels for 22%

profile of v1, /device:TPU:0, one launch (start us, length us, event | category | flops | bytes accessed | tf_op | source)
XLA Modules:
  0.0 662.1 jit_solution(12702623841454050545)
XLA Ops:
  19.5 133.2 %gather_weights.1 = (bf16[2,2,256,1024]{3,2,1,0:T(8,128)(2,1)}, bf16[256,1024]{1,0:T(8,128)(2,1)}, bf16[2,4,2,128,768]{4,3,2,1,0:T(8,128)(2,1)}, bf16[2,4,2,128,...) custom-call(bf16[2,256,1024]{2,1,0:T(8,128)(2,1)} %x_ref.1, ...), custom_call_target="tpu_custom_call" | custom-call | tf_op jit(solution)/shard_map/gather_weights/pallas_call | solution.py:254
  152.7 2.3 fusion.104
  156.2 1.9 fusion.111
  160.0 1.9 fusion.110
  164.4 2.6 fusion.61
  169.7 2.5 copy.93
  172.2 2.2 pad_maximum_fusion.7
  174.5 24.9 %while.27 = (s32[]{:T(128)}, bf16[2,512,8,64]{1,3,2,0:T(8,128)(2,1)}, f32[2,8,512]{2,1,0:T(8,128)S(1)}, bf16[2,512,8,64]{1,3,2,0:T(8,128)(2,1)}, bf16[1024,8,64]...) while((s32[]{:T(128)}, bf16[2,512,8,64]{1,3,2,0:T(8,128)(2,1)}, ...), condition=%wide.region_4.5_spmd, body=%wide.region_1.4_spmd.sunk | while | flops 1111748608 | bytes 66191540 | solution.py:535
  174.5 3.5 multiply_reduce_fusion.15
  178.0 3.4 fusion.180
  181.5 4.3 fusion.181
  186.8 3.5 multiply_reduce_fusion.15
  190.3 3.4 fusion.180
  193.8 4.3 fusion.181
  199.4 2.7 copy.94
  203.4 2.1 fusion.76
  206.4 2.7 swap_k.7
  212.1 2.7 swap_k.8
  218.2 4.2 fusion.102
  222.5 12.4 %multiply_convert_fusion.2 = (bf16[1024,1024]{1,0:T(8,128)(2,1)S(1)}, f32[1024,1024]{1,0:T(8,128)}, f32[1024,1024]{1,0:T(8,128)}) fusion(f32[1024]{0:T(1024)S(1)} %get-tuple-element.374, bf16[1024,1024]{1,0:T(8,128)(2,1)S(1)} %bitcast.295, bf16[1024,1024]{1,0:T(8,128)(2,1)S(1)} %bitcast.320), kind=kOutput, calls=%fused_computation.65 | convolution fusion | flops 2216689664 | bytes 14684160 | tf_op jit(solution)/shard_map/dot_general | solution.py:470
  234.9 2.4 fusion.112
  237.3 21.0 %multiply_convert_fusion.1 = (bf16[1024,1024]{1,0:T(8,128)(2,1)S(1)}, f32[1024,1024]{1,0:T(8,128)}, f32[1024,1024]{1,0:T(8,128)}) fusion(f32[1024]{0:T(1024)S(1)} %get-tuple-element.373, bf16[1024,1024]{1,0:T(8,128)(2,1)S(1)} %bitcast.296, bf16[1024,1024]{1,0:T(8,128)(2,1)S(1)} %bitcast.316), kind=kOutput, calls=%fused_computation.52 | convolution fusion | flops 2216689664 | bytes 14684160 | tf_op jit(solution)/shard_map/dot_general | solution.py:470
  259.6 2.4 convolution_add_fusion.3
  262.2 2.7 swap_k.9
  271.2 3.0 multiply_reduce_fusion.2
  275.8 2.7 swap_k.10
  280.5 3.8 convolution_convert_fusion.2
  284.3 3.7 convolution_convert_fusion.3
  289.1 4.6 convert_reduce_fusion.1
  293.7 3.7 convolution_convert_fusion.1
  297.4 2.4 fusion.113
  301.4 4.3 convert_reduce_fusion
  305.8 4.2 convolution_convert_fusion
  309.9 2.5 convolution_add_fusion.2
  312.6 2.7 swap_k.11
  319.1 2.7 swap_k.12
  329.6 2.4 copy.102
  332.0 75.7 %while.28 = (s32[]{:T(128)}, f32[1024,8,64]{0,2,1:T(8,128)}, f32[1024,8,64]{0,2,1:T(8,128)}, bf16[2,512,8,64]{1,3,2,0:T(8,128)(2,1)}, bf16[2,512,8,64]{1,3,2,0:T...) while((s32[]{:T(128)}, f32[1024,8,64]{0,2,1:T(8,128)}, ...), condition=%wide.region_16.17_spmd.clone, body=%wide.region_14.16_spmd.clone.sunk | while | flops 2737565696 | bytes 195150096 | solution.py:581
  332.3 2.4 fusion.191
  334.6 4.5 bitcast_add_fusion.9
  339.1 9.6 %multiply_reduce_fusion.16 = (f32[8,512]{1,0:T(8,128)S(1)}, f32[8,512,1024]{2,1,0:T(8,128)}) fusion(f32[8,512,1024]{2,1,0:T(8,128)S(1)} %fusion.191, f32[8,512]{1,0:T(8,128)S(1)} %dynamic-slice_bitcast_fusion.2, bf16[1024,8,64]{0,2,1:T(8,128)(2,1)} %get-tuple-element.540, bf16[2,512,8,64]{1,3,2,0:T(8,128)(2,1)} %get-tuple-element.539, s32[]{:T(128)S(6)} %copy.144), kind=kOutput, calls=%fused_computation.15.clone.1 | convolution fusion | flops 553644032 | bytes 35160068 | tf_op jit(solution)/shard_map/while/body/eval_jaxpr/qhd,khd->hqk/dot_general | solution.py:454
  348.8 10.4 %multiply_convert_fusion.4 = bf16[8,512,1024]{2,1,0:T(8,128)(2,1)} fusion(f32[8,512,1024]{2,1,0:T(8,128)} %get-tuple-element.487, f32[8,512,1024]{2,1,0:T(8,128)S(1)} %fusion.191, f32[8,512]{1,0:T(8,128)S(1)} %get-tuple-element.488, f32[8,512]{1,0:T(8,128)S(1)} %dynamic-slice_bitcast_fusion.2), kind=kLoop, calls=%fused_computation.14.clone.1 | loop fusion | flops 20971520 | bytes 41975808 | tf_op jit(solution)/shard_map/while/body/eval_jaxpr/convert_element_type | solution.py:457
  359.2 7.0 %fusion.192 = bf16[2,512,8,64]{1,3,2,0:T(8,128)(2,1)} fusion(bf16[2,512,8,64]{1,3,2,0:T(8,128)(2,1)} %get-tuple-element.524, s32[]{:T(128)S(6)} %copy.144, bf16[8,512,1024]{2,1,0:T(8,128)(2,1)} %multiply_convert_fusion.4, bf16[1024,8,64]{0,2,1:T(8,128)(2,1)S(1)} %get-tuple-element.537), kind=kOutput, calls=%fused_computation.25.clone.1 | convolution fusion | flops 537133056 | bytes 10485764 | tf_op jit(solution)/shard_map/while/body/eval_jaxpr/hqk,khd->qhd/dot_general | solution.py:460
  369.4 2.4 fusion.191
  371.8 5.7 bitcast_add_fusion.9
  377.4 9.6 %multiply_reduce_fusion.16 = (f32[8,512]{1,0:T(8,128)S(1)}, f32[8,512,1024]{2,1,0:T(8,128)}) fusion(f32[8,512,1024]{2,1,0:T(8,128)S(1)} %fusion.191, f32[8,512]{1,0:T(8,128)S(1)} %dynamic-slice_bitcast_fusion.2, bf16[1024,8,64]{0,2,1:T(8,128)(2,1)} %get-tuple-element.540, bf16[2,512,8,64]{1,3,2,0:T(8,128)(2,1)} %get-tuple-element.539, s32[]{:T(128)S(6)} %copy.144), kind=kOutput, calls=%fused_computation.15.clone.1 | convolution fusion | flops 553644032 | bytes 35160068 | tf_op jit(solution)/shard_map/while/body/eval_jaxpr/qhd,khd->hqk/dot_general | solution.py:454
  387.1 10.4 %multiply_convert_fusion.4 = bf16[8,512,1024]{2,1,0:T(8,128)(2,1)} fusion(f32[8,512,1024]{2,1,0:T(8,128)} %get-tuple-element.487, f32[8,512,1024]{2,1,0:T(8,128)S(1)} %fusion.191, f32[8,512]{1,0:T(8,128)S(1)} %get-tuple-element.488, f32[8,512]{1,0:T(8,128)S(1)} %dynamic-slice_bitcast_fusion.2), kind=kLoop, calls=%fused_computation.14.clone.1 | loop fusion | flops 20971520 | bytes 41975808 | tf_op jit(solution)/shard_map/while/body/eval_jaxpr/convert_element_type | solution.py:457
  397.5 7.0 %fusion.192 = bf16[2,512,8,64]{1,3,2,0:T(8,128)(2,1)} fusion(bf16[2,512,8,64]{1,3,2,0:T(8,128)(2,1)} %get-tuple-element.524, s32[]{:T(128)S(6)} %copy.144, bf16[8,512,1024]{2,1,0:T(8,128)(2,1)} %multiply_convert_fusion.4, bf16[1024,8,64]{0,2,1:T(8,128)(2,1)S(1)} %get-tuple-element.537), kind=kOutput, calls=%fused_computation.25.clone.1 | convolution fusion | flops 537133056 | bytes 10485764 | tf_op jit(solution)/shard_map/while/body/eval_jaxpr/hqk,khd->qhd/dot_general | solution.py:460
  407.7 3.4 copy.103
  411.1 2.0 convert_element_type.207
  413.5 1.9 convert_element_type.210
  416.3 3.1 convolution_convert_fusion.4
  420.3 3.0 convolution_convert_fusion.5
  427.2 2.7 swap_k.13
  432.1 4.7 pad_maximum_fusion.refs_0_
  436.8 2.4 pad_maximum_fusion.1.refs_1_
  441.1 1.9 pad_maximum_fusion.2.refs_3_
  443.0 123.7 %reduce_gradients.1 = (f32[128,1024]{1,0:T(8,128)}, f32[128,1024]{1,0:T(8,128)}, f32[128,256]{1,0:T(8,128)}, f32[128,768]{1,0:T(8,128)}) custom-call(bf16[2,4,2,128,1024]{4,3,2,1,0:T(8,128)(2,1)} %pad_maximum_fusion.refs_0_, bf16[2,4,2,128,1024]{4,3,2,1,0:T(8,128)(2,1)} %pad_maximum_fusion.1.refs_1_, bf16[2,4,2,128,256]{4,3,2,1,0:T(8,128)(2,1)} %pad_maximum_fusion.9.refs_2_, ...), custom_call_target="tpu_custom_call" | custom-call | tf_op jit(solution)/shard_map/reduce_gradients/pallas_call | solution.py:393
  577.2 42.5 %all-reduce = (f32[]{:T(128)}, f32[12,1024]{1,0:T(8,128)S(1)}) all-reduce(f32[]{:T(128)S(6)} %add.422, f32[12,1024]{1,0:T(8,128)S(1)} %concatenate.31), channel_id=1, replica_groups=mesh['dp'=8,'mp'=4] {'dp','mp'}, use_global_device_ids=true, to_apply=%region_21.22 | all-reduce | flops 12289 | bytes 98312 | tf_op jit(solution)/shard_map/psum | solution.py:642
  623.7 12.9 %swap_y.1 = bf16[256,1024]{1,0:T(8,128)(2,1)S(1)} custom-call(bf16[256,1024]{1,0:T(8,128)(2,1)S(1)} %fusion.72.src), custom_call_target="tpu_custom_call" | custom-call | tf_op jit(solution)/shard_map/swap_y/pallas_call | solution.py:415
  638.5 1.9 multiply_subtract_fusion.3
  640.4 2.9 multiply_subtract_fusion
  647.4 1.9 copy.110
  649.3 1.9 copy.111
  (334 shorter events, 91.6 us)
Async XLA Ops:
  7.2 11.5 %copy-start = (f32[2,256,1024]{2,1,0:T(8,128)S(1)}, f32[2,256,1024]{2,1,0:T(8,128)}, u32[]{:S(2)}) copy-start(f32[2,256,1024]{2,1,0:T(8,128)} %param.23) | copy-start | bytes 6291460
  7.2 645.0 %reduce-scatter.4.cloned.1.call-start = ((), (), s32[]{:S(2)}) async-start(), calls=%async_computation.1 | async-start | bytes 655360
  17.8 137.2 %copy-start.20 = (f32[128,3,256]{0,2,1:T(8,128)}, f32[128,3,256]{0,2,1:T(8,128)S(1)}, u32[]{:S(2)}) copy-start(f32[128,3,256]{0,2,1:T(8,128)S(1)} %copy.90) | copy-start | bytes 1179652
  152.7 3.5 copy-start.57
  155.0 3.1 copy-start.45
  155.0 4.9 copy-start.47
  169.6 4.8 copy-start.33
  169.7 4.8 copy-start.34
  178.0 3.5 copy-start.15
  178.0 3.5 copy-start.54
  190.3 3.5 copy-start.15
  190.3 3.5 copy-start.54
  199.4 6.1 copy-start.3
  199.4 6.1 copy-start.67
  206.3 2.9 copy-start.58
  206.3 2.9 copy-start.83
  218.2 4.2 copy-start.25
  222.4 12.5 %copy-start.41 = (bf16[1,4,2,128,1024]{4,3,2,1,0:T(8,128)(2,1)}, bf16[1,4,2,128,1024]{4,3,2,1,0:T(8,128)(2,1)S(1)}, u32[]{:S(2)}) copy-start(bf16[1,4,2,128,1024]{4,3,2,1,0:T(8,128)(2,1)S(1)} %get-tuple-element.385) | copy-start | bytes 6291460
  222.4 12.5 %copy-start.43 = (bf16[1,4,2,128,1024]{4,3,2,1,0:T(8,128)(2,1)}, bf16[1,4,2,128,1024]{4,3,2,1,0:T(8,128)(2,1)S(1)}, u32[]{:S(2)}) copy-start(bf16[1,4,2,128,1024]{4,3,2,1,0:T(8,128)(2,1)S(1)} %get-tuple-element.344) | copy-start | bytes 6291460
  222.4 14.8 %copy-start.37 = (bf16[1,4,2,128,1024]{4,3,2,1,0:T(8,128)(2,1)}, bf16[1,4,2,128,1024]{4,3,2,1,0:T(8,128)(2,1)S(1)}, u32[]{:S(2)}) copy-start(bf16[1,4,2,128,1024]{4,3,2,1,0:T(8,128)(2,1)S(1)} %get-tuple-element.386) | copy-start | bytes 6291460
  222.4 35.8 %copy-start.39 = (bf16[1,4,2,128,1024]{4,3,2,1,0:T(8,128)(2,1)}, bf16[1,4,2,128,1024]{4,3,2,1,0:T(8,128)(2,1)S(1)}, u32[]{:S(2)}) copy-start(bf16[1,4,2,128,1024]{4,3,2,1,0:T(8,128)(2,1)S(1)} %get-tuple-element.343) | copy-start | bytes 6291460
  262.0 2.9 copy-start.9
  262.0 2.9 copy-start.80
  269.9 4.4 copy-start.13
  280.5 3.8 copy-start.92
  284.3 3.7 copy-start.44
  284.3 3.7 copy-start.97
  284.3 4.8 copy-start.98
  289.1 4.6 copy-start.26
  293.7 3.7 copy-start.42
  297.4 4.0 copy-start.96
  305.8 4.2 copy-start.38
  327.9 4.1 copy-start.4
  327.9 4.1 copy-start.11
  327.9 4.1 copy-start.68
  359.2 7.0 %copy-start.2 = (bf16[8,512,1024]{2,1,0:T(8,128)(2,1)S(1)}, bf16[8,512,1024]{2,1,0:T(8,128)(2,1)}, u32[]{:S(2)}) copy-start(bf16[8,512,1024]{2,1,0:T(8,128)(2,1)} %multiply_convert_fusion.4) | copy-start | bytes 25165828 | tf_op jit(solution)/shard_map/while
  359.2 7.0 %copy-start.5 = (f32[1024,8,64]{0,2,1:T(8,128)S(1)}, f32[1024,8,64]{0,2,1:T(8,128)}, u32[]{:S(2)}) copy-start(f32[1024,8,64]{0,2,1:T(8,128)} %get-tuple-element.522) | copy-start | bytes 6291460 | tf_op jit(solution)/shard_map/while
  397.5 7.0 %copy-start.2 = (bf16[8,512,1024]{2,1,0:T(8,128)(2,1)S(1)}, bf16[8,512,1024]{2,1,0:T(8,128)(2,1)}, u32[]{:S(2)}) copy-start(bf16[8,512,1024]{2,1,0:T(8,128)(2,1)} %multiply_convert_fusion.4) | copy-start | bytes 25165828 | tf_op jit(solution)/shard_map/while
  397.5 7.0 %copy-start.5 = (f32[1024,8,64]{0,2,1:T(8,128)S(1)}, f32[1024,8,64]{0,2,1:T(8,128)}, u32[]{:S(2)}) copy-start(f32[1024,8,64]{0,2,1:T(8,128)} %get-tuple-element.522) | copy-start | bytes 6291460 | tf_op jit(solution)/shard_map/while
  407.7 5.5 copy-start.7
  420.2 3.0 copy-start.48
  427.0 2.9 copy-start.17
  427.0 2.9 copy-start.74
  432.1 4.7 copy-start.35
  432.1 4.7 copy-start.36
  436.8 3.5 copy-start.50
  443.0 133.2 %copy-start.75 = (f32[1024]{0:T(1024)S(1)}, f32[1024]{0:T(1024)}, u32[]{:S(2)}) copy-start(f32[1024]{0:T(1024)} %get-tuple-element.353) | copy-start | bytes 12292
  443.0 133.2 %copy-start.76 = (f32[1024]{0:T(1024)S(1)}, f32[1024]{0:T(1024)}, u32[]{:S(2)}) copy-start(f32[1024]{0:T(1024)} %get-tuple-element.271) | copy-start | bytes 12292
  443.0 133.2 %copy-start.77 = (f32[1024]{0:T(1024)S(1)}, f32[1024]{0:T(1024)}, u32[]{:S(2)}) copy-start(f32[1024]{0:T(1024)} %get-tuple-element.274) | copy-start | bytes 12292
  443.0 133.2 %copy-start.78 = (f32[1024]{0:T(1024)S(1)}, f32[1024]{0:T(1024)}, u32[]{:S(2)}) copy-start(f32[1024]{0:T(1024)} %get-tuple-element.355) | copy-start | bytes 12292
  443.0 133.2 %copy-start.81 = (f32[1024]{0:T(1024)S(1)}, f32[1024]{0:T(1024)}, u32[]{:S(2)}) copy-start(f32[1024]{0:T(1024)} %get-tuple-element.269) | copy-start | bytes 12292
  443.0 133.2 %copy-start.82 = (f32[1024]{0:T(1024)S(1)}, f32[1024]{0:T(1024)}, u32[]{:S(2)}) copy-start(f32[1024]{0:T(1024)} %get-tuple-element.273) | copy-start | bytes 12292
  443.0 133.3 %copy-start.65 = (f32[128,3,256]{2,0,1:T(8,128)S(1)}, f32[128,3,256]{2,0,1:T(8,128)}, u32[]{:S(2)}) copy-start(f32[128,3,256]{2,0,1:T(8,128)} %param.31) | copy-start | bytes 1179652
  576.3 64.0 %copy-start.30 = (f32[128,1024]{1,0:T(8,128)S(1)}, f32[128,1024]{1,0:T(8,128)}, u32[]{:S(2)}) copy-start(f32[128,1024]{1,0:T(8,128)} %param.28) | copy-start | bytes 1572868
  619.7 3.0 copy-start.66
  636.6 6.7 %copy-start.31 = (f32[128,1024]{1,0:T(8,128)S(1)}, f32[128,1024]{1,0:T(8,128)}, u32[]{:S(2)}) copy-start(f32[128,1024]{1,0:T(8,128)} %param.27) | copy-start | bytes 1572868
  636.6 6.7 %copy-start.32 = (f32[128,1024]{1,0:T(8,128)S(1)}, f32[128,1024]{1,0:T(8,128)}, u32[]{:S(2)}) copy-start(f32[128,1024]{1,0:T(8,128)} %get-tuple-element.123) | copy-start | bytes 1572868
  636.6 6.7 %copy-start.60 = (f32[128,1024]{1,0:T(8,128)S(1)}, f32[128,1024]{1,0:T(8,128)}, u32[]{:S(2)}) copy-start(f32[128,1024]{1,0:T(8,128)} %param.34) | copy-start | bytes 1572868
  636.6 6.7 %copy-start.61 = (f32[128,1024]{1,0:T(8,128)S(1)}, f32[128,1024]{1,0:T(8,128)}, u32[]{:S(2)}) copy-start(f32[128,1024]{1,0:T(8,128)} %param.35) | copy-start | bytes 1572868
  640.4 4.4 copy-start.21
  640.4 4.4 copy-start.51
  640.4 4.4 copy-start.52
  644.7 9.0 %copy-start.1 = (f32[2,256,1024]{2,1,0:T(8,128)S(1)}, f32[2,256,1024]{2,1,0:T(8,128)}, u32[]{:S(2)}) copy-start(f32[2,256,1024]{2,1,0:T(8,128)} %param.23) | copy-start | bytes 6291460
  645.9 5.3 copy-start.53
  (43 other events, 79.6 us)
Sparse Core Ops, SparseCore 0:
  269.9 20.6 reduce-scatter.3
